TPU v7x, 32 devices: a whole 2x2x4 slice. The times are simulated.
32 devices in a mesh: groups: 2 (over x), frame: 8 (over z, y), tok: 2 (over core).
Axes of the slice: x: 2, y: 2, z: 4, core: 2. Of those that a mesh axis runs over, the one named last changes fastest.
Arguments:
- video: bfloat16 [32, 512, 1152], P(('groups', 'frame'), 'tok'), parts along dimension 0, may hold values from -6 to 6
- regions: int32 [32, 512], P(('groups', 'frame'), 'tok'), parts along dimension 0, may hold values from 0 to 2
- prev_frame: int32 [32], P('groups'), parts along dimension 0, may hold values from 0 to 14, as said below
- gain_spatial: float32 [1152], replicated, may hold values from 0.7 to 4
- qkv_spatial: bfloat16 [1152, 3456], replicated, may hold values from -0.35355339 to 0.35355339
- out_spatial: bfloat16 [1152, 1152], replicated, may hold values from -1.5 to 1.5
- gain_temporal: float32 [1152], replicated, may hold values from 0.7 to 4
- qkv_temporal: bfloat16 [1152, 3456], replicated, may hold values from -0.35355339 to 0.35355339
- out_temporal: bfloat16 [1152, 1152], replicated, may hold values from -0.75 to 0.75
Outputs:
- result: bfloat16 [32, 512, 1152], P(('groups', 'frame'), 'tok'), parts along dimension 0
There are 2 independent parts, one for each index of `groups`. A program takes and returns all parts, laid end to end along the dimension named above; an argument that names none is the same for every part. Nothing has to cross between parts.
Inputs may be any that keep to these rules, and one draw needn't show every extreme that they name: prev_frame[f] is f - 1 or f - 2 for 2 <= f < 15, f - 1 for f = 15, and 0 for f < 2.
All inputs are finite; a program needn't handle non-finite values.
Results may differ from a plain program's by a relative error of at most 0.014.
The roundings to bfloat16 on the way count: a program that leaves them out, or rounds other values in their place, can miss the bound.
Values may be sent and summed in bfloat16 or wider, within the bound.
A program may use at most 192 MiB of HBM per device.

v0:
```python
import jax
import jax.numpy as jnp
from jax import lax
from jax.sharding import PartitionSpec as P

HEADS = 16


def from_root(value, axis, source):
    kept = jnp.where(lax.axis_index(axis) == source, value, 0).astype(value.dtype)
    return lax.psum(kept, axis)


def shifted(array, axis, by):
    count = lax.axis_size(axis)
    pairs = [(i, i + by) for i in range(count) if 0 <= i + by < count]
    return lax.ppermute(array, axis, pairs)


def layer_norm(row_data, gain_vector):
    values = row_data.astype(jnp.float32)
    center = values - jnp.mean(values, axis=-1, keepdims=True)
    spread = jnp.mean(center * center, axis=-1, keepdims=True)
    return (center * lax.rsqrt(spread + 1e-06) * gain_vector).astype(jnp.bfloat16)


def softmax_rows(scores, visible):
    masked = jnp.where(visible, scores, -jnp.inf)
    largest = jnp.max(masked, axis=-1, keepdims=True)
    exponent = jnp.exp(masked - largest)
    return (exponent / jnp.sum(exponent, axis=-1, keepdims=True)).astype(jnp.bfloat16)


def temporal_attend(packed_t, flag_rows, score_scale):
    frame_total = packed_t.shape[0]
    query_t = packed_t[:, :, 0]
    key_t = packed_t[:, :, 1]
    value_t = packed_t[:, :, 2]
    scores_t = (
        jnp.einsum("fphd,gphd->phfg", query_t, key_t, preferred_element_type=jnp.float32)
        * score_scale
    )
    open_flag = (flag_rows > 0).T
    visible_t = open_flag[:, None, None, :] | jnp.eye(frame_total, dtype=jnp.bool_)[None, None]
    weights_t = softmax_rows(scores_t, visible_t)
    return jnp.einsum(
        "phfg,gphd->fphd", weights_t, value_t, preferred_element_type=jnp.float32
    ).astype(jnp.bfloat16)


def shards(
    video,
    regions,
    prev_frame,
    gain_spatial,
    qkv_spatial,
    out_spatial,
    gain_temporal,
    qkv_temporal,
    out_temporal,
):
    frames, places, feature = video.shape
    head_size = feature // HEADS
    score_scale = head_size ** (-0.5)
    row_count = frames * places
    normed = layer_norm(video.reshape(row_count, feature), gain_spatial)
    packed = jnp.dot(normed, qkv_spatial, preferred_element_type=jnp.float32).astype(jnp.bfloat16)
    packed = packed.reshape(frames, places, 3 * feature)
    queries = packed[:, :, :feature]
    keys_own = packed[:, :, feature : 2 * feature]
    values_own = packed[:, :, 2 * feature :]
    keep_flag = (regions == 0).astype(jnp.bfloat16)
    key_all, value_all, keep_all = (
        lax.all_gather(keys_own, "tok", axis=1, tiled=True),
        lax.all_gather(values_own, "tok", axis=1, tiled=True),
        lax.all_gather(keep_flag, "tok", axis=1, tiled=True),
    )
    key_first, value_first, keep_first = (
        from_root(key_all[0:1], "frame", 0),
        from_root(value_all[0:1], "frame", 0),
        from_root(keep_all[0:1], "frame", 0),
    )
    key_tail, value_tail, keep_tail = shifted((key_all, value_all, keep_all), "frame", 1)
    whole_places = key_all.shape[1]
    first_index = lax.axis_index("frame") * frames
    own_frames = first_index + jnp.arange(frames, dtype=jnp.int32)
    table_index = jnp.arange(prev_frame.shape[0], dtype=jnp.int32)
    picked = jnp.sum(
        jnp.where(table_index[None, :] == own_frames[:, None], prev_frame[None, :], 0), axis=1
    )
    source_slot = picked - first_index + 2
    key_prev = jnp.take(jnp.concatenate([key_tail, key_all], axis=0), source_slot, axis=0)
    value_prev = jnp.take(jnp.concatenate([value_tail, value_all], axis=0), source_slot, axis=0)
    keep_prev = jnp.take(jnp.concatenate([keep_tail, keep_all], axis=0), source_slot, axis=0)
    ones_row = jnp.ones((whole_places,), jnp.bfloat16)
    attended_list = []
    for local_frame in range(frames):
        key_rows = jnp.concatenate(
            [key_all[local_frame], key_first[0], key_prev[local_frame]], axis=0
        )
        value_rows = jnp.concatenate(
            [value_all[local_frame], value_first[0], value_prev[local_frame]], axis=0
        )
        flag_rows = jnp.concatenate([ones_row, keep_first[0], keep_prev[local_frame]])
        query_rows = queries[local_frame].reshape(places, HEADS, head_size)
        key_rows = key_rows.reshape(3 * whole_places, HEADS, head_size)
        value_rows = value_rows.reshape(3 * whole_places, HEADS, head_size)
        scores = (
            jnp.einsum("qhd,khd->hqk", query_rows, key_rows, preferred_element_type=jnp.float32)
            * score_scale
        )
        weights = softmax_rows(scores, (flag_rows > 0)[None, None, :])
        attended_list.append(
            jnp.einsum(
                "hqk,khd->qhd", weights, value_rows, preferred_element_type=jnp.float32
            ).astype(jnp.bfloat16)
        )
    attended = jnp.stack(attended_list, axis=0).reshape(row_count, feature)
    mixed_rows = (
        video.reshape(row_count, feature).astype(jnp.float32)
        + jnp.dot(attended, out_spatial, preferred_element_type=jnp.float32)
    ).astype(jnp.bfloat16)
    open_flag = (regions != 2).astype(jnp.bfloat16)
    mixed_grid = mixed_rows.reshape(frames, places, feature)
    rows_t, flags_t = (
        lax.all_to_all(mixed_grid, "frame", split_axis=1, concat_axis=0, tiled=True),
        lax.all_to_all(open_flag, "frame", split_axis=1, concat_axis=0, tiled=True),
    )
    frame_total, narrow = (rows_t.shape[0], rows_t.shape[1])
    flat_rows = rows_t.reshape(frame_total * narrow, feature)
    normed_t = layer_norm(flat_rows, gain_temporal)
    packed_t = jnp.dot(normed_t, qkv_temporal, preferred_element_type=jnp.float32).astype(
        jnp.bfloat16
    )
    packed_t = packed_t.reshape(frame_total, narrow, 3, HEADS, head_size)
    temporal_out = temporal_attend(packed_t, flags_t, score_scale).reshape(
        frame_total * narrow, feature
    )
    finished = (
        flat_rows.astype(jnp.float32)
        + jnp.dot(temporal_out, out_temporal, preferred_element_type=jnp.float32)
    ).astype(jnp.bfloat16)
    finished = finished.reshape(frame_total, narrow, feature)
    return lax.all_to_all(finished, "frame", split_axis=0, concat_axis=1, tiled=True)


def solution(mesh):
    placed = (
        P(("groups", "frame"), "tok", None),
        P(("groups", "frame"), "tok"),
        P("groups"),
        P(),
        P(),
        P(),
        P(),
        P(),
        P(),
    )
    return jax.shard_map(
        shards,
        mesh=mesh,
        in_specs=placed,
        out_specs=P(("groups", "frame"), "tok", None),
        check_vma=False,
    )
```

profile of v0, /device:TPU:16, one launch (start us, length us, event | category | flops | bytes accessed | tf_op | source)
XLA Modules:
  0.0 466.7 jit_solution(14256838642502783985)
XLA Ops:
  10.4 8.4 %convolution_convert_fusion.1 = bf16[512,3456]{1,0:T(8,128)(2,1)S(1)} fusion(bf16[512,1152]{1,0:T(8,128)(2,1)S(1)} %fusion.37, bf16[1152,3456]{1,0:T(8,128)(2,1)} %param.15), kind=kOutput, calls=%fused_computation.23 | convolution fusion | flops 4078632960 | bytes 12681216 | tf_op jit(solution)/shard_map/dot_general | solution.py:67
  22.2 1.8 all_gather.10
  24.0 3.4 collective-permute-start.1
  28.1 5.2 %all-to-all-start.1 = ((bf16[2,8,32]{2,0,1:T(2,128)(2,1)}), bf16[2,8,32]{2,0,1:T(2,128)(2,1)S(1)}, u32[]{:S(2)}, u32[]{:S(2)}) async-start(bf16[2,8,32]{2,0,1:T(2,128)(2,1)} %copy.89), calls=%async_computation.1 | async-start | bytes 8192 | tf_op jit(solution)/shard_map/all_to_all | solution.py:127
  33.5 2.1 fusion.89
  35.7 3.4 collective-permute-start
  39.1 8.5 %all-gather.5.cloned.1.call-done = bf16[2,512,1152]{2,1,0:T(8,128)(2,1)} async-done(((bf16[2,256,1152]{2,1,0:T(8,128)(2,1)}), bf16[2,512,1152]{2,1,0:T(8,128)(2,1)}) %all-gather.5.cloned.1.call-update) | async-done | bytes 2359312 | tf_op jit(solution)/shard_map/all_gather | solution.py:74
  47.6 3.4 collective-permute-start.2
  51.0 2.1 copy.76
  54.1 96.1 %psum.22 = bf16[512]{0:T(512)(128)(2,1)S(1)} all-reduce(bf16[512]{0:T(512)(128)(2,1)S(1)} %fusion.70), channel_id=1, replica_groups=mesh['groups'=2,'frame'=8,'tok'=2] {'frame'}, use_global_device_ids=true, to_apply=%region_4.6 | all-reduce | flops 512 | bytes 2048 | tf_op jit(solution)/shard_map/psum | solution.py:11
  151.0 3.6 fusion.93
  154.6 2.4 copy.78
  157.0 3.6 fusion.91
  160.6 2.4 copy.74
  163.0 2.5 copy.77
  165.5 2.5 copy.73
  167.9 2.4 copy.83
  170.4 2.4 copy.80
  172.8 5.0 %pad_maximum_fusion = bf16[4,512,1152]{2,1,0:T(8,128)(2,1)} fusion(bf16[2,512,1152]{2,1,0:T(8,128)(2,1)} %all-gather.3.cloned.1.call-done, bf16[2,512,1152]{2,1,0:T(8,128)(2,1)} %collective-permute-done), kind=kLoop, calls=%fused_computation.24 | loop fusion | flops 2359296 | bytes 9437184 | tf_op jit(solution)/shard_map/concatenate | solution.py:93
  177.8 4.6 gather_fusion.1
  182.4 5.0 %pad_maximum_fusion.1 = bf16[4,512,1152]{2,1,0:T(8,128)(2,1)} fusion(bf16[2,512,1152]{2,1,0:T(8,128)(2,1)} %all-gather.5.cloned.1.call-done, bf16[2,512,1152]{2,1,0:T(8,128)(2,1)} %collective-permute-done.2), kind=kLoop, calls=%fused_computation.25 | loop fusion | flops 2359296 | bytes 9437184 | tf_op jit(solution)/shard_map/concatenate | solution.py:92
  187.4 4.6 gather_fusion.2
  192.0 3.0 broadcast_select_fusion.1
  194.9 2.3 fusion.92
  197.3 2.4 copy.79
  199.7 2.4 copy.75
  202.1 2.4 copy.84
  204.4 2.4 copy.81
  206.8 76.1 %all-reduce.3.cloned.1.call-done = (bf16[512,16,72]{0,2,1:T(8,128)(2,1)}, bf16[512,16,72]{0,2,1:T(8,128)(2,1)}) async-done(((bf16[512,16,72]{0,2,1:T(8,128)(2,1)}, bf16[512,16,72]{0,2,1:T(8,128)(2,1)}), (bf16[512,16,72]{0,2,1:T(8,128)(2,1)}, bf16[512,16,72]{0,2,1:T(8,128)(2,1)})) %all-reduce.3.cloned.1.call-update) | async-done | bytes 2359312 | tf_op jit(solution)/shard_map/psum | solution.py:11
  282.9 13.8 %fusion.98 = (f32[16,256]{1,0:T(8,128)S(1)}, f32[16,256,1536]{2,1,0:T(8,128)}) fusion(pred[1536]{0:T(1024)(128)(4,1)S(1)} %get-tuple-element.31, bf16[256,16,72]{0,2,1:T(8,128)(2,1)} %bitcast.120, bf16[512,16,72]{0,2,1:T(8,128)(2,1)} %get-tuple-element.8, bf16[512,16,72]{0,2,1:T(8,128)(2,1)} %bitcast.117, bf16[512,16,72]{0,2,1:T(8,128)(2,1)} %bitcast.113), kind=kOutput, calls=%fused_computation.136 | convolution fusion | flops 941753856 | bytes 29312512 | tf_op jit(solution)/shard_map/sub | solution.py:30
  296.7 13.8 %fusion.95 = (f32[16,256]{1,0:T(8,128)S(1)}, f32[16,256,1536]{2,1,0:T(8,128)}) fusion(pred[1536]{0:T(1024)(128)(4,1)S(1)} %get-tuple-element.32, bf16[256,16,72]{0,2,1:T(8,128)(2,1)S(1)} %bitcast.119, bf16[512,16,72]{0,2,1:T(8,128)(2,1)} %get-tuple-element.8, bf16[512,16,72]{0,2,1:T(8,128)(2,1)} %bitcast.116, bf16[512,16,72]{0,2,1:T(8,128)(2,1)} %bitcast.112), kind=kOutput, calls=%fused_computation.135 | convolution fusion | flops 941753856 | bytes 29312512 | tf_op jit(solution)/shard_map/sub | solution.py:30
  310.5 11.6 %fusion.62 = bf16[1,256,16,72]{1,3,2,0:T(8,128)(2,1)S(1)} fusion(f32[16,256,1536]{2,1,0:T(8,128)} %get-tuple-element.41, f32[16,256]{1,0:T(8,128)S(1)} %get-tuple-element.40, bf16[512,16,72]{0,2,1:T(8,128)(2,1)} %get-tuple-element.9, bf16[512,16,72]{0,2,1:T(8,128)(2,1)} %bitcast.115, bf16[512,16,72]{0,2,1:T(8,128)(2,1)} %bitcast.110), kind=kOutput, calls=%fused_computation.78 | convolution fusion | flops 929464320 | bytes 29310976 | tf_op jit(solution)/shard_map/hqk,khd->qhd/dot_general | solution.py:114
  322.2 12.5 %fusion.65 = bf16[1,256,16,72]{1,3,2,0:T(8,128)(2,1)} fusion(f32[16,256,1536]{2,1,0:T(8,128)} %get-tuple-element.39, f32[16,256]{1,0:T(8,128)S(1)} %get-tuple-element.38, bf16[512,16,72]{0,2,1:T(8,128)(2,1)} %get-tuple-element.9, bf16[512,16,72]{0,2,1:T(8,128)(2,1)} %bitcast.114, bf16[512,16,72]{0,2,1:T(8,128)(2,1)} %bitcast.111), kind=kOutput, calls=%fused_computation.79 | convolution fusion | flops 929464320 | bytes 29310976 | tf_op jit(solution)/shard_map/hqk,khd->qhd/dot_general | solution.py:114
  337.3 1.9 fusion.28
  339.3 2.2 copy.86
  341.5 5.9 %all-to-all-start = ((bf16[2,256,1152]{2,0,1:T(2,128)(2,1)}), bf16[2,256,1152]{2,0,1:T(2,128)(2,1)}, u32[]{:S(2)}, u32[]{:S(2)}) async-start(bf16[2,256,1152]{2,0,1:T(2,128)(2,1)} %copy.86), calls=%async_computation | async-start | bytes 2359296 | tf_op jit(solution)/shard_map/all_to_all | solution.py:126
  347.7 24.7 %all-to-all-done = bf16[2,256,1152]{2,0,1:T(2,128)(2,1)} async-done(((bf16[2,256,1152]{2,0,1:T(2,128)(2,1)}), bf16[2,256,1152]{2,0,1:T(2,128)(2,1)}, u32[]{:S(2)}, u32[]{:S(2)}) %all-to-all-start) | async-done | bytes 1179680 | tf_op jit(solution)/shard_map/all_to_all | solution.py:126
  372.4 2.1 bitcast_convert_fusion
  378.6 9.7 %convolution_convert_fusion = bf16[512,3456]{1,0:T(8,128)(2,1)} fusion(bf16[512,1152]{1,0:T(8,128)(2,1)S(1)} %fusion.32, bf16[1152,3456]{1,0:T(8,128)(2,1)} %param.18), kind=kOutput, calls=%fused_computation.22 | convolution fusion | flops 4078632960 | bytes 12681216 | tf_op jit(solution)/shard_map/dot_general | solution.py:132
  388.3 13.7 %reshape.236 = bf16[16,32,3,16,72]{4,3,2,1,0:T(8,128)(2,1)} reshape(bf16[512,3456]{1,0:T(8,128)(2,1)} %convolution_convert_fusion) | data formatting | bytes 7077888 | tf_op jit(solution)/shard_map/reshape | solution.py:135
  402.0 4.8 %fusion.88 = (bf16[16,32,1,16,72]{4,3,2,1,0:T(8,128)(2,1)S(1)}, bf16[16,32,1,16,72]{4,3,2,1,0:T(8,128)(2,1)S(1)}, bf16[16,32,1,16,72]{4,3,2,1,0:T(8,128)(2,1)S(1)}) fusion(bf16[16,32,3,16,72]{4,3,2,1,0:T(8,128)(2,1)} %reshape.236), kind=kLoop, calls=%fused_computation.128 | loop fusion | bytes 7077888 | tf_op jit(solution)/shard_map/slice | solution.py:38
  406.8 2.5 fusion.39
  409.3 2.7 fusion.101
  412.0 1.8 convert_bitcast_fusion
  413.8 1.9 copy.94
  415.7 4.6 reshape.237
  420.3 4.7 fusion.29
  424.9 33.7 %all_to_all.45 = bf16[16,32,1152]{2,1,0:T(8,128)(2,1)S(1)} all-to-all(bf16[16,32,1152]{2,1,0:T(8,128)(2,1)S(1)} %bitcast.118), channel_id=1, replica_groups=mesh['groups'=2,'frame'=8,'tok'=2] {'frame'}, dimensions={0} | all-to-all | bytes 2359296 | tf_op jit(solution)/shard_map/all_to_all | solution.py:144
  (73 shorter events, 17.9 us)
Async XLA Ops:
  6.5 330.8 %copy-start = (bf16[1152,1152]{1,0:T(8,128)(2,1)S(1)}, bf16[1152,1152]{1,0:T(8,128)(2,1)}, u32[]{:S(2)}) copy-start(bf16[1152,1152]{1,0:T(8,128)(2,1)} %param.16) | copy-start | bytes 7962628
  6.5 3.4 copy-start.6
  6.5 29.1 %all-gather.3.cloned.1.call-start = ((), (), s32[]{:S(2)}) async-start(), calls=%async_computation.3 | async-start | bytes 3538944 | tf_op jit(solution)/shard_map/all_gather | solution.py:75
  6.5 3.4 copy-start.1
  18.8 2.5 copy-start.4
  21.4 0.8 copy-start.8
  21.4 11.9 %copy-start.9 = (s32[16]{0:T(128)S(1)}, s32[16]{0:T(128)}, u32[]{:S(2)}) copy-start(s32[16]{0:T(128)} %param.13) | copy-start | bytes 196
  21.4 26.2 %all-gather.5.cloned.1.call-start = ((), (), s32[]{:S(2)}) async-start(), calls=%async_computation.4 | async-start | bytes 3538944 | tf_op jit(solution)/shard_map/all_gather | solution.py:74
  24.0 126.3 %collective-permute-start.1 = (bf16[2,512]{1,0:T(2,128)(2,1)S(1)}, bf16[2,512]{1,0:T(2,128)(2,1)S(1)}, u32[]{:S(2)}, u32[]{:S(2)}) collective-permute-start(bf16[2,512]{1,0:T(2,128)(2,1)S(1)} %all_gather.10), channel_id=1, source_target_pairs={{0,2},{2,4},{4,6},{6,8},{8,10},{10,12},{12,14},{1,3},{3,5},{5,7},{... | collective-permute-start | bytes 6152 | tf_op jit(solution)/shard_map/ppermute | solution.py:17
  28.1 313.4 %all-to-all-start.1 = ((bf16[2,8,32]{2,0,1:T(2,128)(2,1)}), bf16[2,8,32]{2,0,1:T(2,128)(2,1)S(1)}, u32[]{:S(2)}, u32[]{:S(2)}) async-start(bf16[2,8,32]{2,0,1:T(2,128)(2,1)} %copy.89), calls=%async_computation.1 | async-start | bytes 8192 | tf_op jit(solution)/shard_map/all_to_all | solution.py:127
  33.3 249.6 %all-reduce.3.cloned.1.call-start = ((), (), s32[]{:S(2)}) async-start(), calls=%async_computation.5 | async-start | bytes 4718592 | tf_op jit(solution)/shard_map/psum | solution.py:11
  35.7 137.1 %collective-permute-start = (bf16[2,512,1152]{2,1,0:T(8,128)(2,1)}, bf16[2,512,1152]{2,1,0:T(8,128)(2,1)}, u32[]{:S(2)}, u32[]{:S(2)}) collective-permute-start(bf16[2,512,1152]{2,1,0:T(8,128)(2,1)} %all-gather.3.cloned.1.call-done), channel_id=1, source_target_pairs={{0,2},{2,4},{4,6},{6,8},{8,10},{10,12},{12,14},{1,3},{3,5},{5,7},{... | collective-permute-start | bytes 7077896 | tf_op jit(solution)/shard_map/ppermute | solution.py:17
  47.6 134.8 %collective-permute-start.2 = (bf16[2,512,1152]{2,1,0:T(8,128)(2,1)}, bf16[2,512,1152]{2,1,0:T(8,128)(2,1)}, u32[]{:S(2)}, u32[]{:S(2)}) collective-permute-start(bf16[2,512,1152]{2,1,0:T(8,128)(2,1)} %all-gather.5.cloned.1.call-done), channel_id=1, source_target_pairs={{0,2},{2,4},{4,6},{6,8},{8,10},{10,12},{12,14},{1,3},{3,5},{5,7},{... | collective-permute-start | bytes 7077896 | tf_op jit(solution)/shard_map/ppermute | solution.py:17
  282.9 13.8 %copy-start.5 = (bf16[1,256,1152]{1,2,0:T(8,128)(2,1)S(1)}, bf16[1,256,1152]{1,2,0:T(8,128)(2,1)}, u32[]{:S(2)}) copy-start(bf16[1,256,1152]{1,2,0:T(8,128)(2,1)} %copy.82) | copy-start | bytes 1769476
  335.8 1.5 copy-start.2
  341.5 30.9 %all-to-all-start = ((bf16[2,256,1152]{2,0,1:T(2,128)(2,1)}), bf16[2,256,1152]{2,0,1:T(2,128)(2,1)}, u32[]{:S(2)}, u32[]{:S(2)}) async-start(bf16[2,256,1152]{2,0,1:T(2,128)(2,1)} %copy.86), calls=%async_computation | async-start | bytes 2359296 | tf_op jit(solution)/shard_map/all_to_all | solution.py:126
  375.1 3.1 copy-start.7
  376.8 1.4 copy-start.3
Sparse Core Ops, SparseCore 0:
  21.5 12.2 all-gather.2
  35.4 12.1 all-gather.4
  172.9 109.9 all-reduce.2
where the time goes:
time: 475 us; the launch traced here: 467 us
  blocking collectives  132 us (28%)
  waiting for transfers between devices  110 us (23%)
  matrix products  80.7 us (17%)
  local copies, waits for them, and re-layouts  77.8 us (16%)
  other arithmetic  31.2 us (7%)
  starting transfers between devices  21.3 us (4%)
  between operations  13.9 us (3%)
    psum x1, blocking collectives, from_root(): return lax.psum(kept, axis)  96.1 us
    psum x1, waiting for transfers between devices, from_root(): return lax.psum(kept, axis)  76.1 us
    all_to_all x1, blocking collectives, shards(): lax.all_to_all(finished, 'frame', split_axis=0, concat_axis=1, tiled=True)  33.7 us
    sub x2, matrix products, softmax_rows(): exponent = jnp.exp(masked - largest)  27.6 us
    all_to_all x1, waiting for transfers between devices, shards(): lax.all_to_all(mixed_grid, 'frame', split_axis=1, concat_axis=0, tiled=True)  24.7 us
    dot_general x2, matrix products, shards(): jnp.einsum('hqk,khd->qhd', weights, value_rows, preferred_element_type=jn...  24.1 us
    reshape x1, local copies, waits for them, and re-layouts, shards(): packed_t = packed_t.reshape(frame_total, narrow, 3, HEADS, head_size)  13.7 us
    ppermute x3, starting transfers between devices, shifted(): return lax.ppermute(array, axis, pairs)  10.1 us
  transfers between devices with their start and end apart: 8, of which 3 were waited for; matrix products, arithmetic and copies ran while one was open for 26% of the time, Pallas kernels for 0%

commit v1 on v0

v1 whole, which is shorter than its diff:
```python
import functools
import math

import jax
import jax.numpy as jnp
from jax import lax
from jax.experimental import pallas as pl
from jax.experimental.pallas import tpu as pltpu
from jax.sharding import PartitionSpec as P

HEADS = 16
WINDOW = 256
VMEM_BYTES = 56 * 1024 * 1024
NT = (((1,), (1,)), ((), ()))


def shifted(array, axis, by):
    count = lax.axis_size(axis)
    pairs = [(i, i + by) for i in range(count) if 0 <= i + by < count]
    return lax.ppermute(array, axis, pairs)


def from_root(value, axis):
    count = lax.axis_size(axis)
    index = lax.axis_index(axis)
    stride = count // 2
    while stride >= 1:
        pairs = [(i, i + stride) for i in range(0, count, 2 * stride) if i + stride < count]
        arrived = lax.ppermute(value, axis, pairs)
        value = jnp.where(index % (2 * stride) == stride, arrived, value)
        stride //= 2
    return value


def normalize(values, gain):
    center = values - jnp.mean(values, axis=-1, keepdims=True)
    spread = jnp.mean(center * center, axis=-1, keepdims=True)
    return (center * lax.rsqrt(spread + 1e-06) * gain).astype(jnp.bfloat16)


def layer_norm(row_data, gain_vector):
    return normalize(row_data.astype(jnp.float32), gain_vector)


def head_window(head, feature):
    size = feature // HEADS
    start = jnp.minimum((head * size) // 128 * 128, feature - WINDOW)
    start = pl.multiple_of(start, 128)
    column = lax.broadcasted_iota(jnp.int32, (1, WINDOW), 1) + start
    inside = (column >= head * size) & (column < (head + 1) * size)
    return start, inside


def spatial_kernel(
    slots, q_ref, own_ref, first_ref, prem_ref, pown_ref, bfirst_ref, bprev_ref,
    video_ref, wout_ref, out_ref, att_ref, *, scale
):
    feature = video_ref.shape[-1]
    frame = pl.program_id(0)
    remote = slots[frame] < 2
    bias_first = bfirst_ref[0]
    bias_prev = bprev_ref[0]
    att_ref[...] = jnp.zeros_like(att_ref)

    def one(head):
        start, inside = head_window(head, feature)
        cols = pl.ds(start, WINDOW)
        vcols = pl.ds(pl.multiple_of(start + feature, 128), WINDOW)
        q = q_ref[0, :, cols]
        q = jnp.where(inside, q, jnp.zeros_like(q))

        def prev(c):
            return jnp.where(remote, prem_ref[0, :, c], pown_ref[0, :, c])

        dot = functools.partial(
            lax.dot_general, dimension_numbers=NT, preferred_element_type=jnp.float32
        )
        s0 = dot(q, own_ref[0, :, cols]) * scale
        s1 = dot(q, first_ref[0, :, cols]) * scale + bias_first
        s2 = dot(q, prev(cols)) * scale + bias_prev
        m = jnp.max(jnp.maximum(jnp.maximum(s0, s1), s2), axis=-1, keepdims=True)
        p0, p1, p2 = jnp.exp2(s0 - m), jnp.exp2(s1 - m), jnp.exp2(s2 - m)
        total = jnp.sum(p0 + p1 + p2, axis=-1, keepdims=True)
        mul = functools.partial(jnp.dot, preferred_element_type=jnp.float32)
        o = (
            mul(p0.astype(jnp.bfloat16), own_ref[0, :, vcols])
            + mul(p1.astype(jnp.bfloat16), first_ref[0, :, vcols])
            + mul(p2.astype(jnp.bfloat16), prev(vcols))
        ) / total
        att_ref[:, cols] = jnp.where(inside, o.astype(jnp.bfloat16), att_ref[:, cols])

    def pair(i, _):
        one(2 * i)
        one(2 * i + 1)
        return 0

    lax.fori_loop(0, HEADS // 2, pair, 0)
    out_ref[0] = (
        video_ref[0].astype(jnp.float32)
        + jnp.dot(att_ref[...], wout_ref[...], preferred_element_type=jnp.float32)
    ).astype(jnp.bfloat16)


def spatial(slots, packed, kv_own, kv_rem, bias_first, bias_prev, video, wout, scale):
    frames, places, feature = video.shape
    whole = kv_own.shape[1]
    kv = (1, whole, 2 * feature)
    return pl.pallas_call(
        functools.partial(spatial_kernel, scale=scale),
        grid_spec=pltpu.PrefetchScalarGridSpec(
            num_scalar_prefetch=1,
            grid=(frames,),
            in_specs=[
                pl.BlockSpec((1, places, feature), lambda f, s: (f, 0, 0)),
                pl.BlockSpec(kv, lambda f, s: (f, 0, 0)),
                pl.BlockSpec(kv, lambda f, s: (2, 0, 0)),
                pl.BlockSpec(kv, lambda f, s: (jnp.minimum(s[f], 1), 0, 0)),
                pl.BlockSpec(kv, lambda f, s: (jnp.maximum(s[f] - 2, 0), 0, 0)),
                pl.BlockSpec((1, 1, whole), lambda f, s: (0, 0, 0)),
                pl.BlockSpec((1, 1, whole), lambda f, s: (f, 0, 0)),
                pl.BlockSpec((1, places, feature), lambda f, s: (f, 0, 0)),
                pl.BlockSpec((feature, feature), lambda f, s: (0, 0)),
            ],
            out_specs=pl.BlockSpec((1, places, feature), lambda f, s: (f, 0, 0)),
            scratch_shapes=[pltpu.VMEM((places, feature), jnp.bfloat16)],
        ),
        out_shape=jax.ShapeDtypeStruct(video.shape, jnp.bfloat16),
        compiler_params=pltpu.CompilerParams(vmem_limit_bytes=VMEM_BYTES),
        cost_estimate=pl.CostEstimate(
            flops=frames * HEADS * 12 * places * whole * WINDOW,
            bytes_accessed=20 << 20,
            transcendentals=frames * HEADS * places * whole * 3,
        ),
    )(slots, packed, kv_own, kv_rem, kv_rem, kv_own, bias_first, bias_prev, video, wout)


def temporal_rows(rows, open_row, gain, wqkv_ref, wout_ref, pack_ref, mask_ref, att_ref, width, scale):
    count, feature = rows.shape
    normed = normalize(rows.astype(jnp.float32), gain)
    for c in range(3):
        cols = pl.ds(c * feature, feature)
        pack_ref[:, cols] = jnp.dot(
            normed, wqkv_ref[:, cols], preferred_element_type=jnp.float32
        ).astype(jnp.bfloat16)
    i = lax.broadcasted_iota(jnp.int32, (count, count), 0)
    j = lax.broadcasted_iota(jnp.int32, (count, count), 1)
    visible = (i % width == j % width) & ((open_row > 0) | (i == j))
    mask_ref[...] = jnp.where(visible, 0.0, -jnp.inf)
    att_ref[...] = jnp.zeros_like(att_ref)

    def one(head):
        start, inside = head_window(head, feature)
        cols = pl.ds(start, WINDOW)
        kcols = pl.ds(pl.multiple_of(start + feature, 128), WINDOW)
        vcols = pl.ds(pl.multiple_of(start + 2 * feature, 128), WINDOW)
        q = pack_ref[:, cols]
        q = jnp.where(inside, q, jnp.zeros_like(q))
        s = lax.dot_general(
            q, pack_ref[:, kcols], dimension_numbers=NT, preferred_element_type=jnp.float32
        )
        s = s * scale + mask_ref[...]
        p = jnp.exp2(s - jnp.max(s, axis=-1, keepdims=True))
        o = jnp.dot(
            p.astype(jnp.bfloat16), pack_ref[:, vcols], preferred_element_type=jnp.float32
        ) / jnp.sum(p, axis=-1, keepdims=True)
        att_ref[:, cols] = jnp.where(inside, o.astype(jnp.bfloat16), att_ref[:, cols])

    def pair(k, _):
        one(2 * k)
        one(2 * k + 1)
        return 0

    lax.fori_loop(0, HEADS // 2, pair, 0)
    return (
        rows.astype(jnp.float32)
        + jnp.dot(att_ref[...], wout_ref[...], preferred_element_type=jnp.float32)
    ).astype(jnp.bfloat16)


def temporal_kernel(
    rows_ref, open_ref, gain_ref, wqkv_ref, wout_ref, out_ref, pack_ref, mask_ref, att_ref,
    *, width, scale
):
    out_ref[...] = temporal_rows(
        rows_ref[...], open_ref[...], gain_ref[...], wqkv_ref, wout_ref,
        pack_ref, mask_ref, att_ref, width, scale,
    )


def temporal(rows, open_row, gain, wqkv, wout, width, scale):
    count, feature = rows.shape
    return pl.pallas_call(
        functools.partial(temporal_kernel, width=width, scale=scale),
        in_specs=[pl.BlockSpec(memory_space=pltpu.VMEM)] * 5,
        out_specs=pl.BlockSpec(memory_space=pltpu.VMEM),
        out_shape=jax.ShapeDtypeStruct(rows.shape, jnp.bfloat16),
        scratch_shapes=[
            pltpu.VMEM((count, 3 * feature), jnp.bfloat16),
            pltpu.VMEM((count, count), jnp.float32),
            pltpu.VMEM((count, feature), jnp.bfloat16),
        ],
        compiler_params=pltpu.CompilerParams(vmem_limit_bytes=VMEM_BYTES),
        cost_estimate=pl.CostEstimate(
            flops=8 * count * feature * feature, bytes_accessed=12 << 20, transcendentals=0
        ),
    )(rows, open_row, gain, wqkv, wout)


def shards(
    video,
    regions,
    prev_frame,
    gain_spatial,
    qkv_spatial,
    out_spatial,
    gain_temporal,
    qkv_temporal,
    out_temporal,
):
    frames, places, feature = video.shape
    devices = lax.axis_size("frame")
    toks = lax.axis_size("tok")
    total_frames = devices * frames
    whole = toks * places
    scale = (feature // HEADS) ** (-0.5) * math.log2(math.e)

    tail = shifted(video, "frame", 1)
    first = from_root(video[0:1], "frame")
    regions_all = lax.all_gather(regions, ("frame", "tok"), axis=0, tiled=False)
    regions_all = regions_all.reshape(devices, toks, frames, places)
    regions_all = regions_all.transpose(0, 2, 1, 3).reshape(total_frames, whole)

    normed = layer_norm(video.reshape(frames * places, feature), gain_spatial)
    packed = jnp.dot(normed, qkv_spatial, preferred_element_type=jnp.float32).astype(jnp.bfloat16)
    packed = packed.reshape(frames, places, 3 * feature)
    kv_own = lax.all_gather(packed[:, :, feature:], "tok", axis=1, tiled=True)

    remote = jnp.concatenate([tail, first], axis=0)
    normed_r = layer_norm(remote.reshape((frames + 1) * places, feature), gain_spatial)
    kv_rem = jnp.dot(
        normed_r, qkv_spatial[:, feature:], preferred_element_type=jnp.float32
    ).astype(jnp.bfloat16)
    kv_rem = kv_rem.reshape(frames + 1, places, 2 * feature)
    kv_rem = lax.all_gather(kv_rem, "tok", axis=1, tiled=True)

    first_index = lax.axis_index("frame") * frames
    picked = lax.dynamic_slice_in_dim(prev_frame, first_index, frames)
    slots = jnp.clip(picked - first_index + 2, 0, 3).astype(jnp.int32)
    keep_bias = jnp.where(regions_all == 0, 0.0, -jnp.inf).astype(jnp.float32)
    bias_first = keep_bias[0:1][:, None]
    bias_prev = jnp.take(keep_bias, picked, axis=0)[:, None]
    mixed = spatial(
        slots, packed, kv_own, kv_rem, bias_first, bias_prev, video, out_spatial, scale
    )

    width = 16 if places % (devices * 16) == 0 else places // devices
    part = devices * width
    chunks = places // part
    my_open = (regions_all != 2).astype(jnp.float32)
    base = lax.axis_index("tok") * places + lax.axis_index("frame") * width
    gain_row = gain_temporal[None]
    done = []
    for c in range(chunks):
        rows = lax.all_to_all(
            mixed[:, c * part : (c + 1) * part], "frame", split_axis=1, concat_axis=0, tiled=True
        )
        open_row = lax.dynamic_slice_in_dim(my_open, base + c * part, width, axis=1)
        finished = temporal(
            rows.reshape(total_frames * width, feature),
            open_row.reshape(1, total_frames * width),
            gain_row, qkv_temporal, out_temporal, width, scale,
        )
        done.append(
            lax.all_to_all(
                finished.reshape(total_frames, width, feature),
                "frame", split_axis=0, concat_axis=1, tiled=True,
            )
        )
    return jnp.concatenate(done, axis=1)


def solution(mesh):
    placed = (
        P(("groups", "frame"), "tok", None),
        P(("groups", "frame"), "tok"),
        P("groups"),
        P(),
        P(),
        P(),
        P(),
        P(),
        P(),
    )
    return jax.shard_map(
        shards,
        mesh=mesh,
        in_specs=placed,
        out_specs=P(("groups", "frame"), "tok", None),
        check_vma=False,
    )
```

time: 475 us -> 251 us (0.53)
  blocking collectives: 132 us -> 17.2 us
  Pallas kernels: 0 us -> 69.3 us
  matrix products: 80.7 us -> 17.2 us
  local copies, waits for them, and re-layouts: 77.8 us -> 14.5 us
  waiting for transfers between devices: 110 us -> 74.2 us
  other arithmetic: 31.2 us -> 6.88 us
  starting transfers between devices: 21.3 us -> 33.7 us
    psum x1 -> x0, blocking collectives: 96.1 us -> none  [from_root(): return lax.psum(kept, axis)]
    psum x1 -> x0, waiting for transfers between devices: 76.1 us -> none  [from_root(): return lax.psum(kept, axis)]
    pallas_call x0 -> x3, Pallas kernels: none -> 69.3 us  [the longest x1 39.6 us: spatial(): pl.pallas_call(functools.partial(spatial_kernel, scale=scale), grid_spec=...]
    ppermute x0 -> x3, waiting for transfers between devices: none -> 49.1 us  [from_root(): arrived = lax.ppermute(value, axis, pairs)]
    dot_general x7 -> x1, matrix products: 44.7 us -> 8.77 us  [shards(): jnp.dot(normed_r, qkv_spatial[:, feature:], preferred_element_type=jnp.fl...]
    all_to_all x1 -> x0, blocking collectives: 33.7 us -> none  [shards(): lax.all_to_all(finished, 'frame', split_axis=0, concat_axis=1, tiled=True)]
    sub x2 -> x0, matrix products: 27.6 us -> none  [softmax_rows(): exponent = jnp.exp(masked - largest)]
    slice x15 -> x5, local copies, waits for them, and re-layouts: 33.6 us -> 6.94 us  [the longest x3 4.18 us: shards(): mixed[:, c * part:(c + 1) * part]]
  transfers between devices with their start and end apart: 8 -> 10, of which waited for: 3 -> 4; matrix products, arithmetic and copies ran while one was open for 26% -> 13% of each run, Pallas kernels for 0% -> 12%
where the time goes in v1:
time: 251 us; the launch traced here: 247 us
  waiting for transfers between devices  74.2 us (30%)
  Pallas kernels  69.3 us (28%)
  starting transfers between devices  33.7 us (13%)
  matrix products  17.2 us (7%)
  blocking collectives  17.2 us (7%)
  local copies, waits for them, and re-layouts  14.5 us (6%)
  between operations  13.7 us (5%)
  other arithmetic  6.88 us (3%)
    ppermute x3, waiting for transfers between devices, from_root(): arrived = lax.ppermute(value, axis, pairs)  49.1 us
    pallas_call x1, Pallas kernels, spatial(): pl.pallas_call(functools.partial(spatial_kernel, scale=scale), grid_spec=...  39.6 us
    pallas_call x2, Pallas kernels, temporal(): pl.pallas_call(functools.partial(temporal_kernel, width=width, scale=scal...  29.7 us
    all_gather x1, blocking collectives, shards(): regions_all = lax.all_gather(regions, ('frame', 'tok'), axis=0, tiled=False)  17.2 us
    all_to_all x2, starting transfers between devices, shards(): lax.all_to_all(mixed[:, c * part:(c + 1) * part], 'frame', split_axis=1,...  14.2 us
    all_to_all x2, waiting for transfers between devices, shards(): lax.all_to_all(finished.reshape(total_frames, width, feature), 'frame', s...  12.7 us
    all_to_all x2, waiting for transfers between devices, shards(): lax.all_to_all(mixed[:, c * part:(c + 1) * part], 'frame', split_axis=1,...  12.3 us
    all_to_all x2, starting transfers between devices, shards(): lax.all_to_all(finished.reshape(total_frames, width, feature), 'frame', s...  12 us
  transfers between devices with their start and end apart: 10, of which 4 were waited for; matrix products, arithmetic and copies ran while one was open for 13% of the time, Pallas kernels for 12%

profile of v1, /device:TPU:16, one launch (start us, length us, event | category | flops | bytes accessed | tf_op | source)
XLA Modules:
  0.0 246.6 jit_solution(10961113971079260603)
XLA Ops:
  6.5 1.2 slice.19
  7.7 1.3 collective-permute-start.1
  9.0 1.5 convert_reduce_fusion
  10.6 0.4 multiply_reduce_fusion.1
  11.1 0.4 fusion.10
  11.5 14.1 %collective-permute-done.1 = bf16[1,256,1152]{2,1,0:T(8,128)(2,1)S(1)} collective-permute-done((bf16[1,256,1152]{2,1,0:T(8,128)(2,1)S(1)}, bf16[1,256,1152]{2,1,0:T(8,128)(2,1)S(1)}, u32[]{:S(2)}, u32[]{:S(2)}) %collective-permute-start.1) | collective-permute-done | bytes 589856 | tf_op jit(solution)/shard_map/ppermute | solution.py:29
  25.6 0.1 broadcast_select_fusion
  25.7 2.1 collective-permute-start.2
  27.8 8.4 %convolution_convert_fusion = bf16[512,3456]{1,0:T(8,128)(2,1)S(1)} fusion(bf16[512,1152]{1,0:T(8,128)(2,1)S(1)} %fusion.10, bf16[1152,3456]{1,0:T(8,128)(2,1)} %param.13), kind=kOutput, calls=%fused_computation.1 | convolution fusion | flops 4078632960 | bytes 12681216 | tf_op jit(solution)/shard_map/dot_general | solution.py:234
  36.2 1.8 copy-done.1
  38.0 1.6 slice.26
  39.6 0.0 all-gather.7.cloned.1.call-start
  39.7 1.9 collective-permute-start
  41.6 0.1 broadcast_select_fusion.1
  41.7 2.1 collective-permute-start.3
  43.8 35.0 %collective-permute-done.3 = bf16[1,256,1152]{2,1,0:T(8,128)(2,1)} collective-permute-done((bf16[1,256,1152]{2,1,0:T(8,128)(2,1)S(1)}, bf16[1,256,1152]{2,1,0:T(8,128)(2,1)}, u32[]{:S(2)}, u32[]{:S(2)}) %collective-permute-start.3) | collective-permute-done | bytes 589856 | tf_op jit(solution)/shard_map/ppermute | solution.py:29
  78.8 0.1 broadcast_select_fusion.2
  78.9 0.3 fusion.11
  79.3 0.6 multiply_reduce_fusion
  79.9 0.2 maximum_convert_fusion
  80.1 0.5 fusion.7
  80.7 8.8 %fusion.2 = bf16[768,2304]{1,0:T(8,128)(2,1)} fusion(bf16[768,1152]{1,0:T(8,128)(2,1)S(1)} %fusion.7, bf16[1152,3456]{1,0:T(8,128)(2,1)} %param.13), kind=kOutput, calls=%fused_computation.4 | convolution fusion | flops 4078632960 | bytes 10616832 | tf_op jit(solution)/shard_map/dot_general | solution.py:240
  89.5 0.6 copy-done.4
  90.1 17.2 %all-gather.1 = s32[16,2,256]{2,1,0:T(2,128)S(1)} all-gather(s32[1,2,256]{2,1,0:T(2,128)S(1)} %bitcast.81), channel_id=2, replica_groups=mesh['groups'=2,'frame'=8,'tok'=2] {'frame','tok'}, dimensions={0}, use_global_device_ids=true | all-gather | bytes 34816 | tf_op jit(solution)/shard_map/all_gather | solution.py:229
  107.4 0.1 compare_and_fusion
  107.5 0.6 gather_fusion
  108.1 0.7 add_clamp_fusion.slots
  108.7 0.7 broadcast_select_fusion.3.bprev_ref
  109.4 0.6 slice_bitcast_fusion.bfirst_ref
  110.0 39.6 %shard_map.91 = bf16[2,256,1152]{2,1,0:T(8,128)(2,1)} custom-call(s32[2]{0:T(128)} %add_clamp_fusion.slots, bf16[2,256,3456]{2,1,0:T(8,128)(2,1)} %bitcast.71, bf16[2,512,2304]{2,1,0:T(8,128)(2,1)} %all-gather.5.cloned.1.call-done.own_ref.pown_ref, bf16[3,512,2304]{2,1,0:T(8,128)(2,1)} %all-gather.7.cloned.1.call-done.first_ref.prem_ref, ...), custom_call_target="tpu_custom_call" | custom-call | flops 12884901888 | bytes 20971520 | tf_op jit(solution)/shard_map/pallas_call | solution.py:108
  149.6 1.3 fusion.13
  151.0 1.4 copy.17
  152.4 7.6 %all-to-all-start = ((bf16[2,128,1152]{2,0,1:T(2,128)(2,1)}), bf16[2,128,1152]{2,0,1:T(2,128)(2,1)S(1)}, u32[]{:S(2)}, u32[]{:S(2)}) async-start(bf16[2,128,1152]{2,0,1:T(2,128)(2,1)} %copy.17), calls=%async_computation | async-start | bytes 1179648 | tf_op jit(solution)/shard_map/all_to_all | solution.py:264
  160.0 1.4 copy.21
  161.4 12.3 %all-to-all-done = bf16[2,128,1152]{2,0,1:T(2,128)(2,1)S(1)} async-done(((bf16[2,128,1152]{2,0,1:T(2,128)(2,1)}), bf16[2,128,1152]{2,0,1:T(2,128)(2,1)S(1)}, u32[]{:S(2)}, u32[]{:S(2)}) %all-to-all-start) | async-done | bytes 589856 | tf_op jit(solution)/shard_map/all_to_all | solution.py:264
  173.7 6.6 %all-to-all-start.2 = ((bf16[2,128,1152]{2,0,1:T(2,128)(2,1)}), bf16[2,128,1152]{2,0,1:T(2,128)(2,1)S(1)}, u32[]{:S(2)}, u32[]{:S(2)}) async-start(bf16[2,128,1152]{2,0,1:T(2,128)(2,1)} %copy.21), calls=%async_computation.2 | async-start | bytes 1179648 | tf_op jit(solution)/shard_map/all_to_all | solution.py:264
  180.3 0.6 broadcast_in_dim.39.gain_ref
  181.0 0.1 constant_dynamic-slice_fusion.1
  181.0 0.7 reshape.149.open_ref
  181.7 0.9 copy.18
  182.6 14.8 %shard_map.92 = bf16[256,1152]{1,0:T(8,128)(2,1)} custom-call(bf16[256,1152]{1,0:T(8,128)(2,1)} %bitcast.63, f32[1,256]{1,0:T(1,128)} %reshape.149.open_ref, f32[1,1152]{1,0:T(1,128)} %broadcast_in_dim.39.gain_ref, bf16[1152,3456]{1,0:T(8,128)(2,1)} %wqkv_ref.3, bf16[1152,1152]{1,0:T(8,128)(2,1)} %wout_ref.5), custom_call_target="tpu_custom_call" | custom-call | flops 2717908992 | bytes 12582912 | tf_op jit(solution)/shard_map/pallas_call | solution.py:192
  197.4 6.0 %all-to-all-start.1 = ((bf16[16,16,1152]{2,1,0:T(8,128)(2,1)}), bf16[16,16,1152]{2,1,0:T(8,128)(2,1)S(1)}, u32[]{:S(2)}, u32[]{:S(2)}) async-start(bf16[16,16,1152]{2,1,0:T(8,128)(2,1)} %bitcast.60), calls=%async_computation.1 | async-start | bytes 1179648 | tf_op jit(solution)/shard_map/all_to_all | solution.py:274
  203.4 0.7 reshape.152.open_ref
  204.1 0.9 copy.22
  205.0 14.9 %shard_map.93 = bf16[256,1152]{1,0:T(8,128)(2,1)} custom-call(bf16[256,1152]{1,0:T(8,128)(2,1)} %bitcast.62, f32[1,256]{1,0:T(1,128)} %reshape.152.open_ref, f32[1,1152]{1,0:T(1,128)} %broadcast_in_dim.39.gain_ref, bf16[1152,3456]{1,0:T(8,128)(2,1)} %wqkv_ref.3, bf16[1152,1152]{1,0:T(8,128)(2,1)} %wout_ref.5), custom_call_target="tpu_custom_call" | custom-call | flops 2717908992 | bytes 12582912 | tf_op jit(solution)/shard_map/pallas_call | solution.py:192
  219.8 6.0 %all-to-all-start.3 = ((bf16[16,16,1152]{2,1,0:T(8,128)(2,1)}), bf16[16,16,1152]{2,1,0:T(8,128)(2,1)S(1)}, u32[]{:S(2)}, u32[]{:S(2)}) async-start(bf16[16,16,1152]{2,1,0:T(8,128)(2,1)} %bitcast.61), calls=%async_computation.3 | async-start | bytes 1179648 | tf_op jit(solution)/shard_map/all_to_all | solution.py:274
  225.9 12.7 %all-to-all-done.3 = bf16[16,16,1152]{2,1,0:T(8,128)(2,1)S(1)} async-done(((bf16[16,16,1152]{2,1,0:T(8,128)(2,1)}), bf16[16,16,1152]{2,1,0:T(8,128)(2,1)S(1)}, u32[]{:S(2)}, u32[]{:S(2)}) %all-to-all-start.3) | async-done | bytes 589856 | tf_op jit(solution)/shard_map/all_to_all | solution.py:274
  238.6 1.1 pad_maximum_fusion
  (36 shorter events, 0.3 us)
Async XLA Ops:
  6.5 4.0 %copy-start = (bf16[2,256,1152]{2,1,0:T(8,128)(2,1)S(1)}, bf16[2,256,1152]{2,1,0:T(8,128)(2,1)}, u32[]{:S(2)}) copy-start(bf16[2,256,1152]{2,1,0:T(8,128)(2,1)} %video_ref.1) | copy-start | bytes 3538948
  6.5 4.5 %copy-start.2 = (f32[1152]{0:T(1024)S(1)}, f32[1152]{0:T(1024)}, u32[]{:S(2)}) copy-start(f32[1152]{0:T(1024)} %param.12) | copy-start | bytes 13828
  6.5 103.4 %all-gather.5.cloned.1.call-start = ((), (), s32[]{:S(2)}) async-start(), calls=%async_computation.4 | async-start | bytes 7077888 | tf_op jit(solution)/shard_map/all_gather | solution.py:236
  7.7 17.9 %collective-permute-start.1 = (bf16[1,256,1152]{2,1,0:T(8,128)(2,1)S(1)}, bf16[1,256,1152]{2,1,0:T(8,128)(2,1)S(1)}, u32[]{:S(2)}, u32[]{:S(2)}) collective-permute-start(bf16[1,256,1152]{2,1,0:T(8,128)(2,1)S(1)} %slice.19), channel_id=1, source_target_pairs={{0,8},{1,9},{16,24},{17,25}} | collective-permute-start | bytes 1769480 | tf_op jit(solution)/shard_map/ppermute | solution.py:29
  25.7 15.9 %collective-permute-start.2 = (bf16[1,256,1152]{2,1,0:T(8,128)(2,1)S(1)}, bf16[1,256,1152]{2,1,0:T(8,128)(2,1)}, u32[]{:S(2)}, u32[]{:S(2)}) collective-permute-start(bf16[1,256,1152]{2,1,0:T(8,128)(2,1)S(1)} %broadcast_select_fusion), channel_id=1, source_target_pairs={{0,4},{8,12},{1,5},{9,13},{16,20},{24,28},{17,21},{25,29}} | collective-permute-start | bytes 1769480 | tf_op jit(solution)/shard_map/ppermute | solution.py:29
  36.2 1.8 copy-start.1
  39.6 70.4 %all-gather.7.cloned.1.call-start = ((), (), s32[]{:S(2)}) async-start(), calls=%async_computation.5 | async-start | bytes 10616832 | tf_op jit(solution)/shard_map/all_gather | solution.py:244
  39.7 39.3 %collective-permute-start = (bf16[2,256,1152]{2,1,0:T(8,128)(2,1)S(1)}, bf16[2,256,1152]{2,1,0:T(8,128)(2,1)S(1)}, u32[]{:S(2)}, u32[]{:S(2)}) collective-permute-start(bf16[2,256,1152]{2,1,0:T(8,128)(2,1)S(1)} %copy-done), channel_id=1, source_target_pairs={{0,2},{2,4},{4,6},{6,8},{8,10},{10,12},{12,14},{1,3},{3,5},{5,7},{... | collective-permute-start | bytes 3538952 | tf_op jit(solution)/shard_map/ppermute | solution.py:20
  41.7 37.1 %collective-permute-start.3 = (bf16[1,256,1152]{2,1,0:T(8,128)(2,1)S(1)}, bf16[1,256,1152]{2,1,0:T(8,128)(2,1)}, u32[]{:S(2)}, u32[]{:S(2)}) collective-permute-start(bf16[1,256,1152]{2,1,0:T(8,128)(2,1)S(1)} %broadcast_select_fusion.1), channel_id=1, source_target_pairs={{0,2},{4,6},{8,10},{12,14},{1,3},{5,7},{9,11},{13,15},{16,18},{20,... | collective-permute-start | bytes 1769480 | tf_op jit(solution)/shard_map/ppermute | solution.py:29
  89.4 0.7 copy-start.4
  89.4 18.0 %copy-start.5 = (s32[16]{0:T(128)S(1)}, s32[16]{0:T(128)}, u32[]{:S(2)}) copy-start(s32[16]{0:T(128)} %param.11) | copy-start | bytes 196
  151.0 29.3 %copy-start.3 = (f32[1152]{0:T(1024)S(1)}, f32[1152]{0:T(1024)}, u32[]{:S(2)}) copy-start(f32[1152]{0:T(1024)} %param.15) | copy-start | bytes 13828
  152.4 21.3 %all-to-all-start = ((bf16[2,128,1152]{2,0,1:T(2,128)(2,1)}), bf16[2,128,1152]{2,0,1:T(2,128)(2,1)S(1)}, u32[]{:S(2)}, u32[]{:S(2)}) async-start(bf16[2,128,1152]{2,0,1:T(2,128)(2,1)} %copy.17), calls=%async_computation | async-start | bytes 1179648 | tf_op jit(solution)/shard_map/all_to_all | solution.py:264
  173.7 23.8 %all-to-all-start.2 = ((bf16[2,128,1152]{2,0,1:T(2,128)(2,1)}), bf16[2,128,1152]{2,0,1:T(2,128)(2,1)S(1)}, u32[]{:S(2)}, u32[]{:S(2)}) async-start(bf16[2,128,1152]{2,0,1:T(2,128)(2,1)} %copy.21), calls=%async_computation.2 | async-start | bytes 1179648 | tf_op jit(solution)/shard_map/all_to_all | solution.py:264
  197.4 22.4 %all-to-all-start.1 = ((bf16[16,16,1152]{2,1,0:T(8,128)(2,1)}), bf16[16,16,1152]{2,1,0:T(8,128)(2,1)S(1)}, u32[]{:S(2)}, u32[]{:S(2)}) async-start(bf16[16,16,1152]{2,1,0:T(8,128)(2,1)} %bitcast.60), calls=%async_computation.1 | async-start | bytes 1179648 | tf_op jit(solution)/shard_map/all_to_all | solution.py:274
  219.8 18.7 %all-to-all-start.3 = ((bf16[16,16,1152]{2,1,0:T(8,128)(2,1)}), bf16[16,16,1152]{2,1,0:T(8,128)(2,1)S(1)}, u32[]{:S(2)}, u32[]{:S(2)}) async-start(bf16[16,16,1152]{2,1,0:T(8,128)(2,1)} %bitcast.61), calls=%async_computation.3 | async-start | bytes 1179648 | tf_op jit(solution)/shard_map/all_to_all | solution.py:274
Sparse Core Ops, SparseCore 0:
  39.7 13.7 all-gather.4
  89.6 20.3 all-gather.6

commit v2 on v1

v2 whole, which is shorter than its diff:
```python
import functools
import math

import jax
import jax.numpy as jnp
from jax import lax
from jax.experimental import pallas as pl
from jax.experimental.pallas import tpu as pltpu
from jax.sharding import PartitionSpec as P

HEADS = 16
WINDOW = 256
VMEM_BYTES = 56 * 1024 * 1024
NT = (((1,), (1,)), ((), ()))


def normalize(values, gain):
    center = values - jnp.mean(values, axis=-1, keepdims=True)
    spread = jnp.mean(center * center, axis=-1, keepdims=True)
    return (center * lax.rsqrt(spread + 1e-06) * gain).astype(jnp.bfloat16)


def head_window(head, feature):
    size = feature // HEADS
    start = jnp.minimum((head * size) // 128 * 128, feature - WINDOW)
    start = pl.multiple_of(start, 128)
    column = lax.broadcasted_iota(jnp.int32, (1, WINDOW), 1) + start
    inside = (column >= head * size) & (column < (head + 1) * size)
    return start, inside


def spatial_kernel(
    slots_ref, video_ref, gain_ref, wqkv_ref, wout_ref, bfirst_ref, bprev_ref, out_ref,
    tail_ref, first_ref, q_ref, own_ref, rem_ref, att_ref,
    scatter_send, spread_send, first_recv, tail_send, tail_recv, kv_send, kv_recv,
    *, devices, scale
):
    frames, places, feature = video_ref.shape
    me = lax.axis_index("frame")
    tok = lax.axis_index("tok")
    piece = places // devices
    mesh_id = pl.DeviceIdType.MESH

    def rows_of(index, size):
        return pl.ds(pl.multiple_of(index * size, size), size)

    mine = rows_of(tok, places)

    barrier = pltpu.get_barrier_semaphore()
    for k in range(1, devices):
        pl.semaphore_signal(
            barrier, inc=1, device_id={"frame": lax.rem(me + k, devices)}, device_id_type=mesh_id
        )
    pl.semaphore_signal(barrier, inc=1, device_id={"tok": 1 - tok}, device_id_type=mesh_id)
    pl.semaphore_wait(barrier, devices)

    def scatter(d):
        return pltpu.make_async_remote_copy(
            src_ref=video_ref.at[0, pl.ds(d * piece, piece)],
            dst_ref=first_ref.at[pl.ds(d * piece, piece)],
            send_sem=scatter_send.at[d],
            recv_sem=first_recv.at[d],
            device_id={"frame": d},
            device_id_type=mesh_id,
        )

    def spread(k):
        return pltpu.make_async_remote_copy(
            src_ref=first_ref.at[rows_of(me, piece)],
            dst_ref=first_ref.at[rows_of(me, piece)],
            send_sem=spread_send.at[k],
            recv_sem=first_recv.at[me],
            device_id={"frame": lax.rem(me + k, devices)},
            device_id_type=mesh_id,
        )

    def arrival(p):
        return pltpu.make_async_remote_copy(
            src_ref=first_ref.at[rows_of(p, piece)],
            dst_ref=first_ref.at[rows_of(p, piece)],
            send_sem=spread_send.at[0],
            recv_sem=first_recv.at[p],
            device_id={"frame": lax.rem(me + 1, devices)},
            device_id_type=mesh_id,
        )

    shift = pltpu.make_async_remote_copy(
        src_ref=video_ref,
        dst_ref=tail_ref,
        send_sem=tail_send,
        recv_sem=tail_recv,
        device_id={"frame": lax.rem(me + 1, devices)},
        device_id_type=mesh_id,
    )

    def swap(ref, index, number):
        return pltpu.make_async_remote_copy(
            src_ref=ref.at[index, mine],
            dst_ref=ref.at[index, mine],
            send_sem=kv_send.at[number],
            recv_sem=kv_recv.at[number],
            device_id={"tok": 1 - tok},
            device_id_type=mesh_id,
        )

    @pl.when(me == 0)
    def _():
        for d in range(1, devices):
            scatter(d).start()
        first_ref[...] = video_ref[0]
        tail_ref[...] = jnp.zeros_like(tail_ref)

    @pl.when(me < devices - 1)
    def _():
        shift.start()

    gain = gain_ref[...]
    keys = pl.ds(feature, feature)
    values = pl.ds(2 * feature, feature)

    def project(normed, cols):
        return jnp.dot(
            normed, wqkv_ref[:, cols], preferred_element_type=jnp.float32
        ).astype(jnp.bfloat16)

    def send_kv(rows, ref, index, number):
        normed = normalize(rows.astype(jnp.float32), gain)
        ref[index, mine, pl.ds(0, feature)] = project(normed, keys)
        ref[index, mine, pl.ds(feature, feature)] = project(normed, values)
        swap(ref, index, number).start()
        return normed

    for f in range(frames):
        normed = send_kv(video_ref[f], own_ref, f, f)
        q_ref[f] = project(normed, pl.ds(0, feature))
        if f == 0:
            @pl.when(me > 0)
            def _():
                arrival(me).wait_recv()

            for k in range(1, devices):
                @pl.when(lax.rem(me + k, devices) != 0)
                def _():
                    spread(k).start()

    @pl.when(me > 0)
    def _():
        shift.wait_recv()

    for f in range(frames):
        send_kv(tail_ref[f], rem_ref, f, frames + f)

    @pl.when(me > 0)
    def _():
        for k in range(1, devices):
            arrival(lax.rem(me + k, devices)).wait_recv()

    send_kv(first_ref[...], rem_ref, frames, 2 * frames)

    for f in range(frames):
        swap(own_ref, f, f).wait()
    for f in range(frames + 1):
        swap(rem_ref, f, frames + f).wait()

    bias_first = bfirst_ref[0]
    att_ref[...] = jnp.zeros_like(att_ref)
    dot = functools.partial(
        lax.dot_general, dimension_numbers=NT, preferred_element_type=jnp.float32
    )
    mul = functools.partial(jnp.dot, preferred_element_type=jnp.float32)

    def frame_step(frame, _):
        slot = slots_ref[frame]
        remote = slot < frames
        rem_slot = jnp.minimum(slot, frames - 1)
        own_slot = jnp.maximum(slot - frames, 0)
        bias_prev = bprev_ref[frame]

        def one(head):
            start, inside = head_window(head, feature)
            cols = pl.ds(start, WINDOW)
            vcols = pl.ds(pl.multiple_of(start + feature, 128), WINDOW)
            q = q_ref[frame, :, cols]
            q = jnp.where(inside, q, jnp.zeros_like(q))

            def prev(c):
                return jnp.where(remote, rem_ref[rem_slot, :, c], own_ref[own_slot, :, c])

            s0 = dot(q, own_ref[frame, :, cols]) * scale
            s1 = dot(q, rem_ref[frames, :, cols]) * scale + bias_first
            s2 = dot(q, prev(cols)) * scale + bias_prev
            m = jnp.max(jnp.maximum(jnp.maximum(s0, s1), s2), axis=-1, keepdims=True)
            p0, p1, p2 = jnp.exp2(s0 - m), jnp.exp2(s1 - m), jnp.exp2(s2 - m)
            total = jnp.sum(p0 + p1 + p2, axis=-1, keepdims=True)
            o = (
                mul(p0.astype(jnp.bfloat16), own_ref[frame, :, vcols])
                + mul(p1.astype(jnp.bfloat16), rem_ref[frames, :, vcols])
                + mul(p2.astype(jnp.bfloat16), prev(vcols))
            ) / total
            att_ref[:, cols] = jnp.where(inside, o.astype(jnp.bfloat16), att_ref[:, cols])

        def pair(i, _):
            one(2 * i)
            one(2 * i + 1)
            return 0

        lax.fori_loop(0, HEADS // 2, pair, 0)
        out_ref[frame] = (
            video_ref[frame].astype(jnp.float32)
            + jnp.dot(att_ref[...], wout_ref[...], preferred_element_type=jnp.float32)
        ).astype(jnp.bfloat16)
        return 0

    lax.fori_loop(0, frames, frame_step, 0)

    @pl.when(me == 0)
    def _():
        for d in range(1, devices):
            scatter(d).wait_send()

    @pl.when(me < devices - 1)
    def _():
        shift.wait_send()

    for k in range(1, devices):
        @pl.when(lax.rem(me + k, devices) != 0)
        def _():
            spread(k).wait_send()


def spatial(slots, video, gain, wqkv, wout, bias_first, bias_prev, devices, toks, scale):
    frames, places, feature = video.shape
    whole = toks * places
    vmem = pl.BlockSpec(memory_space=pltpu.VMEM)
    dma = pltpu.SemaphoreType.DMA
    return pl.pallas_call(
        functools.partial(spatial_kernel, devices=devices, scale=scale),
        in_specs=[pl.BlockSpec(memory_space=pltpu.SMEM)] + [vmem] * 6,
        out_specs=vmem,
        out_shape=jax.ShapeDtypeStruct(video.shape, jnp.bfloat16),
        scratch_shapes=[
            pltpu.VMEM((frames, places, feature), jnp.bfloat16),
            pltpu.VMEM((places, feature), jnp.bfloat16),
            pltpu.VMEM((frames, places, feature), jnp.bfloat16),
            pltpu.VMEM((frames, whole, 2 * feature), jnp.bfloat16),
            pltpu.VMEM((frames + 1, whole, 2 * feature), jnp.bfloat16),
            pltpu.VMEM((places, feature), jnp.bfloat16),
            dma((devices,)),
            dma((devices,)),
            dma((devices,)),
            dma,
            dma,
            dma((2 * frames + 1,)),
            dma((2 * frames + 1,)),
        ],
        compiler_params=pltpu.CompilerParams(
            collective_id=0, has_side_effects=True, vmem_limit_bytes=VMEM_BYTES
        ),
        cost_estimate=pl.CostEstimate(
            flops=frames * HEADS * 12 * places * whole * WINDOW,
            bytes_accessed=20 << 20,
            transcendentals=frames * HEADS * places * whole * 3,
        ),
    )(slots, video, gain, wqkv, wout, bias_first, bias_prev)


def temporal_rows(rows, open_row, gain, wqkv_ref, wout_ref, pack_ref, mask_ref, att_ref, width, scale):
    count, feature = rows.shape
    normed = normalize(rows.astype(jnp.float32), gain)
    for c in range(3):
        cols = pl.ds(c * feature, feature)
        pack_ref[:, cols] = jnp.dot(
            normed, wqkv_ref[:, cols], preferred_element_type=jnp.float32
        ).astype(jnp.bfloat16)
    i = lax.broadcasted_iota(jnp.int32, (count, count), 0)
    j = lax.broadcasted_iota(jnp.int32, (count, count), 1)
    visible = (i % width == j % width) & ((open_row > 0) | (i == j))
    mask_ref[...] = jnp.where(visible, 0.0, -jnp.inf)
    att_ref[...] = jnp.zeros_like(att_ref)

    def one(head):
        start, inside = head_window(head, feature)
        cols = pl.ds(start, WINDOW)
        kcols = pl.ds(pl.multiple_of(start + feature, 128), WINDOW)
        vcols = pl.ds(pl.multiple_of(start + 2 * feature, 128), WINDOW)
        q = pack_ref[:, cols]
        q = jnp.where(inside, q, jnp.zeros_like(q))
        s = lax.dot_general(
            q, pack_ref[:, kcols], dimension_numbers=NT, preferred_element_type=jnp.float32
        )
        s = s * scale + mask_ref[...]
        p = jnp.exp2(s - jnp.max(s, axis=-1, keepdims=True))
        o = jnp.dot(
            p.astype(jnp.bfloat16), pack_ref[:, vcols], preferred_element_type=jnp.float32
        ) / jnp.sum(p, axis=-1, keepdims=True)
        att_ref[:, cols] = jnp.where(inside, o.astype(jnp.bfloat16), att_ref[:, cols])

    def pair(k, _):
        one(2 * k)
        one(2 * k + 1)
        return 0

    lax.fori_loop(0, HEADS // 2, pair, 0)
    return (
        rows.astype(jnp.float32)
        + jnp.dot(att_ref[...], wout_ref[...], preferred_element_type=jnp.float32)
    ).astype(jnp.bfloat16)


def temporal_kernel(
    rows_ref, open_ref, gain_ref, wqkv_ref, wout_ref, out_ref, pack_ref, mask_ref, att_ref,
    *, width, scale
):
    out_ref[...] = temporal_rows(
        rows_ref[...], open_ref[...], gain_ref[...], wqkv_ref, wout_ref,
        pack_ref, mask_ref, att_ref, width, scale,
    )


def temporal(rows, open_row, gain, wqkv, wout, width, scale):
    count, feature = rows.shape
    return pl.pallas_call(
        functools.partial(temporal_kernel, width=width, scale=scale),
        in_specs=[pl.BlockSpec(memory_space=pltpu.VMEM)] * 5,
        out_specs=pl.BlockSpec(memory_space=pltpu.VMEM),
        out_shape=jax.ShapeDtypeStruct(rows.shape, jnp.bfloat16),
        scratch_shapes=[
            pltpu.VMEM((count, 3 * feature), jnp.bfloat16),
            pltpu.VMEM((count, count), jnp.float32),
            pltpu.VMEM((count, feature), jnp.bfloat16),
        ],
        compiler_params=pltpu.CompilerParams(vmem_limit_bytes=VMEM_BYTES),
        cost_estimate=pl.CostEstimate(
            flops=8 * count * feature * feature, bytes_accessed=12 << 20, transcendentals=0
        ),
    )(rows, open_row, gain, wqkv, wout)


def shards(
    video,
    regions,
    prev_frame,
    gain_spatial,
    qkv_spatial,
    out_spatial,
    gain_temporal,
    qkv_temporal,
    out_temporal,
):
    frames, places, feature = video.shape
    devices = lax.axis_size("frame")
    toks = lax.axis_size("tok")
    total_frames = devices * frames
    whole = toks * places
    scale = (feature // HEADS) ** (-0.5) * math.log2(math.e)

    regions_all = lax.all_gather(regions, ("frame", "tok"), axis=0, tiled=False)
    regions_all = regions_all.reshape(devices, toks, frames, places)
    regions_all = regions_all.transpose(0, 2, 1, 3).reshape(total_frames, whole)

    first_index = lax.axis_index("frame") * frames
    picked = lax.dynamic_slice_in_dim(prev_frame, first_index, frames)
    slots = jnp.clip(picked - first_index + frames, 0, 2 * frames - 1).astype(jnp.int32)
    keep_bias = jnp.where(regions_all == 0, 0.0, -jnp.inf).astype(jnp.float32)
    bias_first = keep_bias[0:1][:, None]
    bias_prev = jnp.take(keep_bias, picked, axis=0)[:, None]
    mixed = spatial(
        slots, video, gain_spatial[None], qkv_spatial, out_spatial, bias_first, bias_prev,
        devices, toks, scale,
    )

    width = 16 if places % (devices * 16) == 0 else places // devices
    part = devices * width
    chunks = places // part
    my_open = (regions_all != 2).astype(jnp.float32)
    base = lax.axis_index("tok") * places + lax.axis_index("frame") * width
    gain_row = gain_temporal[None]
    done = []
    for c in range(chunks):
        rows = lax.all_to_all(
            mixed[:, c * part : (c + 1) * part], "frame", split_axis=1, concat_axis=0, tiled=True
        )
        open_row = lax.dynamic_slice_in_dim(my_open, base + c * part, width, axis=1)
        finished = temporal(
            rows.reshape(total_frames * width, feature),
            open_row.reshape(1, total_frames * width),
            gain_row, qkv_temporal, out_temporal, width, scale,
        )
        done.append(
            lax.all_to_all(
                finished.reshape(total_frames, width, feature),
                "frame", split_axis=0, concat_axis=1, tiled=True,
            )
        )
    return jnp.concatenate(done, axis=1)


def solution(mesh):
    placed = (
        P(("groups", "frame"), "tok", None),
        P(("groups", "frame"), "tok"),
        P("groups"),
        P(),
        P(),
        P(),
        P(),
        P(),
        P(),
    )
    return jax.shard_map(
        shards,
        mesh=mesh,
        in_specs=placed,
        out_specs=P(("groups", "frame"), "tok", None),
        check_vma=False,
    )
```

time: 251 us -> 204 us (0.81)
  waiting for transfers between devices: 74.2 us -> 24.7 us
  Pallas kernels: 69.3 us -> 115 us
  matrix products: 17.2 us -> 0 us
  between operations: 13.7 us -> 0.08 us
  starting transfers between devices: 33.7 us -> 29.4 us
  local copies, waits for them, and re-layouts: 14.5 us -> 10.5 us
  other arithmetic: 6.88 us -> 3.75 us
    ppermute x4 -> x0, waiting for transfers between devices: 49.1 us -> none  [the longest x3 49.1 us: from_root(): arrived = lax.ppermute(value, axis, pairs)]
    pallas_call x1, Pallas kernels: 39.6 us -> 85.3 us  [spatial(): pl.pallas_call(functools.partial(spatial_kernel, devices=devices, scale=s...]
    dot_general x2 -> x0, matrix products: 17.2 us -> none  [the longest x1 8.77 us: shards(): jnp.dot(normed_r, qkv_spatial[:, feature:], preferred_element_type=jnp.fl...]
    ppermute x4 -> x0, starting transfers between devices: 7.45 us -> none  [the longest x3 5.53 us: from_root(): arrived = lax.ppermute(value, axis, pairs)]
    all_to_all x2, starting transfers between devices: 14.2 us -> 17.4 us  [shards(): lax.all_to_all(mixed[:, c * part:(c + 1) * part], 'frame', split_axis=1,...]
    reduce_sum x4 -> x0, other arithmetic: 2.88 us -> none  [the longest x2 1.81 us: normalize(): center = values - jnp.mean(values, axis=-1, keepdims=True)]
    slice x2 -> x0, local copies, waits for them, and re-layouts: 2.76 us -> none  [the longest x1 1.55 us: shards(): kv_own = lax.all_gather(packed[:, :, feature:], 'tok', axis=1, tiled=True)]
  transfers between devices with their start and end apart: 10 -> 4, of which waited for: 4 -> 2; matrix products, arithmetic and copies ran while one was open for 13% -> 3% of each run, Pallas kernels for 12% -> 15%
where the time goes in v2:
time: 204 us; the launch traced here: 200 us
  Pallas kernels  115 us (56%)
  starting transfers between devices  29.4 us (14%)
  waiting for transfers between devices  24.7 us (12%)
  blocking collectives  16.3 us (8%)
  local copies, waits for them, and re-layouts  10.5 us (5%)
  other arithmetic  3.75 us (2%)
    pallas_call x1, Pallas kernels, spatial(): pl.pallas_call(functools.partial(spatial_kernel, devices=devices, scale=s...  85.3 us
    pallas_call x2, Pallas kernels, temporal(): pl.pallas_call(functools.partial(temporal_kernel, width=width, scale=scal...  29.7 us
    all_to_all x2, starting transfers between devices, shards(): lax.all_to_all(mixed[:, c * part:(c + 1) * part], 'frame', split_axis=1,...  17.4 us
    all_gather x1, blocking collectives, shards(): regions_all = lax.all_gather(regions, ('frame', 'tok'), axis=0, tiled=False)  16.3 us
    all_to_all x2, waiting for transfers between devices, shards(): lax.all_to_all(finished.reshape(total_frames, width, feature), 'frame', s...  12.7 us
    all_to_all x2, waiting for transfers between devices, shards(): lax.all_to_all(mixed[:, c * part:(c + 1) * part], 'frame', split_axis=1,...  12 us
    all_to_all x2, starting transfers between devices, shards(): lax.all_to_all(finished.reshape(total_frames, width, feature), 'frame', s...  12 us
    slice x3, local copies, waits for them, and re-layouts, shards(): mixed[:, c * part:(c + 1) * part]  4.18 us
  transfers between devices with their start and end apart: 4, of which 2 were waited for; matrix products, arithmetic and copies ran while one was open for 3% of the time, Pallas kernels for 15%

profile of v2, /device:TPU:16, one launch (start us, length us, event | category | flops | bytes accessed | tf_op | source)
XLA Modules:
  0.0 199.8 jit_solution(5799910919830665383)
XLA Ops:
  0.0 1.2 add_clamp_fusion.slots_ref
  1.2 0.7 compare_and_fusion
  2.0 1.3 broadcast_in_dim.30.gain_ref
  3.2 16.3 %all-gather.1 = s32[16,2,256]{2,1,0:T(2,128)S(1)} all-gather(s32[1,2,256]{2,1,0:T(2,128)} %bitcast.49), channel_id=2, replica_groups=mesh['groups'=2,'frame'=8,'tok'=2] {'frame','tok'}, dimensions={0}, use_global_device_ids=true | all-gather | bytes 34816 | tf_op jit(solution)/shard_map/all_gather | solution.py:357
  19.6 0.6 slice_bitcast_fusion.bfirst_ref
  20.2 0.6 gather_fusion
  20.7 0.7 broadcast_select_fusion.bprev_ref
  21.4 85.3 %shard_map.91 = bf16[2,256,1152]{2,1,0:T(8,128)(2,1)} custom-call(s32[2]{0:T(128)} %add_clamp_fusion.slots_ref, bf16[2,256,1152]{2,1,0:T(8,128)(2,1)} %video_ref.1, f32[1,1152]{1,0:T(1,128)} %broadcast_in_dim.30.gain_ref, bf16[1152,3456]{1,0:T(8,128)(2,1)} %wqkv_ref.3, bf16[1152,1152]{1,0:T(8,128)(2,1)} %wout_ref.3, ...), custom_call_target="tpu_custom_call" | custom-call | flops 12884901888 | bytes 20971520 | tf_op jit(solution)/shard_map/pallas_call | solution.py:236
  106.8 1.3 fusion
  108.1 0.0 copy-start
  108.1 1.4 copy.17
  109.5 10.8 %all-to-all-start = ((bf16[2,128,1152]{2,0,1:T(2,128)(2,1)}), bf16[2,128,1152]{2,0,1:T(2,128)(2,1)S(1)}, u32[]{:S(2)}, u32[]{:S(2)}) async-start(bf16[2,128,1152]{2,0,1:T(2,128)(2,1)} %copy.17), calls=%async_computation | async-start | bytes 1179648 | tf_op jit(solution)/shard_map/all_to_all | solution.py:380
  120.3 1.4 copy.21
  121.7 12.0 %all-to-all-done = bf16[2,128,1152]{2,0,1:T(2,128)(2,1)S(1)} async-done(((bf16[2,128,1152]{2,0,1:T(2,128)(2,1)}), bf16[2,128,1152]{2,0,1:T(2,128)(2,1)S(1)}, u32[]{:S(2)}, u32[]{:S(2)}) %all-to-all-start) | async-done | bytes 589856 | tf_op jit(solution)/shard_map/all_to_all | solution.py:380
  133.8 6.6 %all-to-all-start.2 = ((bf16[2,128,1152]{2,0,1:T(2,128)(2,1)}), bf16[2,128,1152]{2,0,1:T(2,128)(2,1)S(1)}, u32[]{:S(2)}, u32[]{:S(2)}) async-start(bf16[2,128,1152]{2,0,1:T(2,128)(2,1)} %copy.21), calls=%async_computation.2 | async-start | bytes 1179648 | tf_op jit(solution)/shard_map/all_to_all | solution.py:380
  140.4 0.0 copy-done
  140.4 0.6 broadcast_in_dim.37.gain_ref
  141.0 0.1 constant_dynamic-slice_fusion.1
  141.1 0.7 reshape.70.open_ref
  141.7 0.9 copy.18
  142.6 14.8 %shard_map.92 = bf16[256,1152]{1,0:T(8,128)(2,1)} custom-call(bf16[256,1152]{1,0:T(8,128)(2,1)} %bitcast.35, f32[1,256]{1,0:T(1,128)} %reshape.70.open_ref, f32[1,1152]{1,0:T(1,128)} %broadcast_in_dim.37.gain_ref, bf16[1152,3456]{1,0:T(8,128)(2,1)} %wqkv_ref.5, bf16[1152,1152]{1,0:T(8,128)(2,1)} %wout_ref.5), custom_call_target="tpu_custom_call" | custom-call | flops 2717908992 | bytes 12582912 | tf_op jit(solution)/shard_map/pallas_call | solution.py:322
  157.5 0.0 all-to-all-done.2
  157.5 6.0 %all-to-all-start.1 = ((bf16[16,16,1152]{2,1,0:T(8,128)(2,1)}), bf16[16,16,1152]{2,1,0:T(8,128)(2,1)S(1)}, u32[]{:S(2)}, u32[]{:S(2)}) async-start(bf16[16,16,1152]{2,1,0:T(8,128)(2,1)} %bitcast.32), calls=%async_computation.1 | async-start | bytes 1179648 | tf_op jit(solution)/shard_map/all_to_all | solution.py:390
  163.5 0.7 reshape.73.open_ref
  164.1 0.9 copy.22
  165.0 14.8 %shard_map.93 = bf16[256,1152]{1,0:T(8,128)(2,1)} custom-call(bf16[256,1152]{1,0:T(8,128)(2,1)} %bitcast.34, f32[1,256]{1,0:T(1,128)} %reshape.73.open_ref, f32[1,1152]{1,0:T(1,128)} %broadcast_in_dim.37.gain_ref, bf16[1152,3456]{1,0:T(8,128)(2,1)} %wqkv_ref.5, bf16[1152,1152]{1,0:T(8,128)(2,1)} %wout_ref.5), custom_call_target="tpu_custom_call" | custom-call | flops 2717908992 | bytes 12582912 | tf_op jit(solution)/shard_map/pallas_call | solution.py:322
  179.8 0.0 all-to-all-done.1
  179.8 6.0 %all-to-all-start.3 = ((bf16[16,16,1152]{2,1,0:T(8,128)(2,1)}), bf16[16,16,1152]{2,1,0:T(8,128)(2,1)S(1)}, u32[]{:S(2)}, u32[]{:S(2)}) async-start(bf16[16,16,1152]{2,1,0:T(8,128)(2,1)} %bitcast.33), calls=%async_computation.3 | async-start | bytes 1179648 | tf_op jit(solution)/shard_map/all_to_all | solution.py:390
  185.9 12.7 %all-to-all-done.3 = bf16[16,16,1152]{2,1,0:T(8,128)(2,1)S(1)} async-done(((bf16[16,16,1152]{2,1,0:T(8,128)(2,1)}), bf16[16,16,1152]{2,1,0:T(8,128)(2,1)S(1)}, u32[]{:S(2)}, u32[]{:S(2)}) %all-to-all-start.3) | async-done | bytes 589856 | tf_op jit(solution)/shard_map/all_to_all | solution.py:390
  198.6 1.1 pad_maximum_fusion
  (9 shorter events, 0.2 us)
Async XLA Ops:
  108.1 32.3 %copy-start = (f32[1152]{0:T(1024)S(1)}, f32[1152]{0:T(1024)}, u32[]{:S(2)}) copy-start(f32[1152]{0:T(1024)} %param.15) | copy-start | bytes 13828
  109.5 24.2 %all-to-all-start = ((bf16[2,128,1152]{2,0,1:T(2,128)(2,1)}), bf16[2,128,1152]{2,0,1:T(2,128)(2,1)S(1)}, u32[]{:S(2)}, u32[]{:S(2)}) async-start(bf16[2,128,1152]{2,0,1:T(2,128)(2,1)} %copy.17), calls=%async_computation | async-start | bytes 1179648 | tf_op jit(solution)/shard_map/all_to_all | solution.py:380
  133.8 23.7 %all-to-all-start.2 = ((bf16[2,128,1152]{2,0,1:T(2,128)(2,1)}), bf16[2,128,1152]{2,0,1:T(2,128)(2,1)S(1)}, u32[]{:S(2)}, u32[]{:S(2)}) async-start(bf16[2,128,1152]{2,0,1:T(2,128)(2,1)} %copy.21), calls=%async_computation.2 | async-start | bytes 1179648 | tf_op jit(solution)/shard_map/all_to_all | solution.py:380
  157.5 22.4 %all-to-all-start.1 = ((bf16[16,16,1152]{2,1,0:T(8,128)(2,1)}), bf16[16,16,1152]{2,1,0:T(8,128)(2,1)S(1)}, u32[]{:S(2)}, u32[]{:S(2)}) async-start(bf16[16,16,1152]{2,1,0:T(8,128)(2,1)} %bitcast.32), calls=%async_computation.1 | async-start | bytes 1179648 | tf_op jit(solution)/shard_map/all_to_all | solution.py:390
  179.8 18.7 %all-to-all-start.3 = ((bf16[16,16,1152]{2,1,0:T(8,128)(2,1)}), bf16[16,16,1152]{2,1,0:T(8,128)(2,1)S(1)}, u32[]{:S(2)}, u32[]{:S(2)}) async-start(bf16[16,16,1152]{2,1,0:T(8,128)(2,1)} %bitcast.33), calls=%async_computation.3 | async-start | bytes 1179648 | tf_op jit(solution)/shard_map/all_to_all | solution.py:390

commit v3 on v2

--- a/solution.py
+++ b/solution.py
@@ -30,8 +30,8 @@
 
 
 def spatial_kernel(
-    slots_ref, video_ref, gain_ref, wqkv_ref, wout_ref, bfirst_ref, bprev_ref, out_ref,
-    tail_ref, first_ref, q_ref, own_ref, rem_ref, att_ref,
+    slots_ref, video_ref, gain_ref, wqkv_ref, wout_ref, own_reg_ref, out_ref, reg_out_ref,
+    tail_ref, first_ref, q_ref, own_ref, rem_ref, att_ref, reg_ref, reg_send, reg_recv,
     scatter_send, spread_send, first_recv, tail_send, tail_recv, kv_send, kv_recv,
     *, devices, scale
 ):
@@ -51,8 +51,26 @@
         pl.semaphore_signal(
             barrier, inc=1, device_id={"frame": lax.rem(me + k, devices)}, device_id_type=mesh_id
         )
-    pl.semaphore_signal(barrier, inc=1, device_id={"tok": 1 - tok}, device_id_type=mesh_id)
-    pl.semaphore_wait(barrier, devices)
+    for k in range(devices):
+        pl.semaphore_signal(
+            barrier,
+            inc=1,
+            device_id={"frame": lax.rem(me + k, devices), "tok": 1 - tok},
+            device_id_type=mesh_id,
+        )
+    pl.semaphore_wait(barrier, 2 * devices - 1)
+
+    def tell(j, k):
+        return pltpu.make_async_remote_copy(
+            src_ref=own_reg_ref,
+            dst_ref=reg_ref.at[tok, me],
+            send_sem=reg_send.at[j, k],
+            recv_sem=reg_recv.at[j, k],
+            device_id={"frame": lax.rem(me + k, devices), "tok": tok if j == 0 else 1 - tok},
+            device_id_type=mesh_id,
+        )
+
+    others = [(j, k) for j in range(2) for k in range(devices) if j + k > 0]
 
     def scatter(d):
         return pltpu.make_async_remote_copy(
@@ -114,6 +132,10 @@
     def _():
         shift.start()
 
+    for j, k in others:
+        tell(j, k).start()
+    reg_ref[tok, me] = own_reg_ref[...]
+
     gain = gain_ref[...]
     keys = pl.ds(feature, feature)
     values = pl.ds(2 * feature, feature)
@@ -162,7 +184,15 @@
     for f in range(frames + 1):
         swap(rem_ref, f, frames + f).wait()
 
-    bias_first = bfirst_ref[0]
+    for j, k in others:
+        tell(j, k).wait()
+    reg_out_ref[...] = reg_ref[tok]
+
+    def keep_bias(device, row):
+        flags = jnp.concatenate([reg_ref[0, device, row], reg_ref[1, device, row]], axis=-1)
+        return jnp.where(flags == 0, 0.0, -jnp.inf)
+
+    bias_first = keep_bias(0, 0)
     att_ref[...] = jnp.zeros_like(att_ref)
     dot = functools.partial(
         lax.dot_general, dimension_numbers=NT, preferred_element_type=jnp.float32
@@ -170,11 +200,11 @@
     mul = functools.partial(jnp.dot, preferred_element_type=jnp.float32)
 
     def frame_step(frame, _):
-        slot = slots_ref[frame]
+        slot = slots_ref[0, frame]
         remote = slot < frames
         rem_slot = jnp.minimum(slot, frames - 1)
         own_slot = jnp.maximum(slot - frames, 0)
-        bias_prev = bprev_ref[frame]
+        bias_prev = keep_bias(slots_ref[1, frame], slots_ref[2, frame])
 
         def one(head):
             start, inside = head_window(head, feature)
@@ -228,16 +258,19 @@
             spread(k).wait_send()
 
 
-def spatial(slots, video, gain, wqkv, wout, bias_first, bias_prev, devices, toks, scale):
+def spatial(slots, video, gain, wqkv, wout, own_reg, devices, toks, scale):
     frames, places, feature = video.shape
     whole = toks * places
     vmem = pl.BlockSpec(memory_space=pltpu.VMEM)
     dma = pltpu.SemaphoreType.DMA
     return pl.pallas_call(
         functools.partial(spatial_kernel, devices=devices, scale=scale),
-        in_specs=[pl.BlockSpec(memory_space=pltpu.SMEM)] + [vmem] * 6,
-        out_specs=vmem,
-        out_shape=jax.ShapeDtypeStruct(video.shape, jnp.bfloat16),
+        in_specs=[pl.BlockSpec(memory_space=pltpu.SMEM)] + [vmem] * 5,
+        out_specs=[vmem, vmem],
+        out_shape=[
+            jax.ShapeDtypeStruct(video.shape, jnp.bfloat16),
+            jax.ShapeDtypeStruct((devices, frames, 1, places), jnp.float32),
+        ],
         scratch_shapes=[
             pltpu.VMEM((frames, places, feature), jnp.bfloat16),
             pltpu.VMEM((places, feature), jnp.bfloat16),
@@ -245,6 +278,9 @@
             pltpu.VMEM((frames, whole, 2 * feature), jnp.bfloat16),
             pltpu.VMEM((frames + 1, whole, 2 * feature), jnp.bfloat16),
             pltpu.VMEM((places, feature), jnp.bfloat16),
+            pltpu.VMEM((toks, devices, frames, 1, places), jnp.float32),
+            dma((2, devices)),
+            dma((2, devices)),
             dma((devices,)),
             dma((devices,)),
             dma((devices,)),
@@ -261,7 +297,7 @@
             bytes_accessed=20 << 20,
             transcendentals=frames * HEADS * places * whole * 3,
         ),
-    )(slots, video, gain, wqkv, wout, bias_first, bias_prev)
+    )(slots, video, gain, wqkv, wout, own_reg)
 
 
 def temporal_rows(rows, open_row, gain, wqkv_ref, wout_ref, pack_ref, mask_ref, att_ref, width, scale):
@@ -308,32 +344,98 @@
 
 
 def temporal_kernel(
-    rows_ref, open_ref, gain_ref, wqkv_ref, wout_ref, out_ref, pack_ref, mask_ref, att_ref,
-    *, width, scale
+    mixed_ref, open_ref, gain_ref, wqkv_ref, wout_ref, out_ref,
+    recv_ref, fin_ref, land_ref, pack_ref, mask_ref, att_ref,
+    go_send, go_recv, back_send, back_recv, *, devices, width, scale
 ):
-    out_ref[...] = temporal_rows(
-        rows_ref[...], open_ref[...], gain_ref[...], wqkv_ref, wout_ref,
-        pack_ref, mask_ref, att_ref, width, scale,
-    )
-
-
-def temporal(rows, open_row, gain, wqkv, wout, width, scale):
-    count, feature = rows.shape
+    frames, places, feature = mixed_ref.shape
+    chunks = recv_ref.shape[0]
+    part = devices * width
+    count = part * frames
+    me = lax.axis_index("frame")
+    mesh_id = pl.DeviceIdType.MESH
+
+    barrier = pltpu.get_barrier_semaphore()
+    for k in range(1, devices):
+        pl.semaphore_signal(
+            barrier, inc=1, device_id={"frame": lax.rem(me + k, devices)}, device_id_type=mesh_id
+        )
+    pl.semaphore_wait(barrier, devices - 1)
+
+    def slab(c, device):
+        return pl.ds(pl.multiple_of(c * part + device * width, width), width)
+
+    def go(c, k):
+        target = lax.rem(me + k, devices)
+        return pltpu.make_async_remote_copy(
+            src_ref=mixed_ref.at[:, slab(c, target)],
+            dst_ref=recv_ref.at[c, me],
+            send_sem=go_send.at[c, k],
+            recv_sem=go_recv.at[c, k],
+            device_id={"frame": target},
+            device_id_type=mesh_id,
+        )
+
+    def back(c, k):
+        target = lax.rem(me + k, devices)
+        return pltpu.make_async_remote_copy(
+            src_ref=fin_ref.at[c, target],
+            dst_ref=land_ref.at[:, slab(c, me)],
+            send_sem=back_send.at[c, k],
+            recv_sem=back_recv.at[c, k],
+            device_id={"frame": target},
+            device_id_type=mesh_id,
+        )
+
+    for c in range(chunks):
+        for k in range(1, devices):
+            go(c, k).start()
+        recv_ref[c, me] = mixed_ref[:, slab(c, me)]
+    for c in range(chunks):
+        for k in range(1, devices):
+            go(c, k).wait()
+        finished = temporal_rows(
+            recv_ref[c].reshape(count, feature), open_ref[c], gain_ref[...], wqkv_ref, wout_ref,
+            pack_ref, mask_ref, att_ref, width, scale,
+        )
+        fin_ref[c] = finished.reshape(devices, frames, width, feature)
+        for k in range(1, devices):
+            back(c, k).start()
+        land_ref[:, slab(c, me)] = fin_ref[c, me]
+    for c in range(chunks):
+        for k in range(1, devices):
+            back(c, k).wait()
+    out_ref[...] = land_ref[...]
+
+
+def temporal(mixed, open_rows, gain, wqkv, wout, devices, width, scale):
+    frames, places, feature = mixed.shape
+    chunks, _, count = open_rows.shape
+    vmem = pl.BlockSpec(memory_space=pltpu.VMEM)
+    block = pltpu.VMEM((chunks, devices, frames, width, feature), jnp.bfloat16)
     return pl.pallas_call(
-        functools.partial(temporal_kernel, width=width, scale=scale),
-        in_specs=[pl.BlockSpec(memory_space=pltpu.VMEM)] * 5,
-        out_specs=pl.BlockSpec(memory_space=pltpu.VMEM),
-        out_shape=jax.ShapeDtypeStruct(rows.shape, jnp.bfloat16),
+        functools.partial(temporal_kernel, devices=devices, width=width, scale=scale),
+        in_specs=[vmem] * 5,
+        out_specs=vmem,
+        out_shape=jax.ShapeDtypeStruct(mixed.shape, jnp.bfloat16),
         scratch_shapes=[
+            block,
+            block,
+            pltpu.VMEM(mixed.shape, jnp.bfloat16),
             pltpu.VMEM((count, 3 * feature), jnp.bfloat16),
             pltpu.VMEM((count, count), jnp.float32),
             pltpu.VMEM((count, feature), jnp.bfloat16),
-        ],
-        compiler_params=pltpu.CompilerParams(vmem_limit_bytes=VMEM_BYTES),
+        ]
+        + [pltpu.SemaphoreType.DMA((chunks, devices))] * 4,
+        compiler_params=pltpu.CompilerParams(
+            collective_id=1, has_side_effects=True, vmem_limit_bytes=VMEM_BYTES
+        ),
         cost_estimate=pl.CostEstimate(
-            flops=8 * count * feature * feature, bytes_accessed=12 << 20, transcendentals=0
+            flops=8 * chunks * count * feature * feature,
+            bytes_accessed=16 << 20,
+            transcendentals=0,
         ),
-    )(rows, open_row, gain, wqkv, wout)
+    )(mixed, open_rows, gain, wqkv, wout)
 
 
 def shards(
@@ -354,45 +456,28 @@
     whole = toks * places
     scale = (feature // HEADS) ** (-0.5) * math.log2(math.e)
 
-    regions_all = lax.all_gather(regions, ("frame", "tok"), axis=0, tiled=False)
-    regions_all = regions_all.reshape(devices, toks, frames, places)
-    regions_all = regions_all.transpose(0, 2, 1, 3).reshape(total_frames, whole)
-
     first_index = lax.axis_index("frame") * frames
     picked = lax.dynamic_slice_in_dim(prev_frame, first_index, frames)
     slots = jnp.clip(picked - first_index + frames, 0, 2 * frames - 1).astype(jnp.int32)
-    keep_bias = jnp.where(regions_all == 0, 0.0, -jnp.inf).astype(jnp.float32)
-    bias_first = keep_bias[0:1][:, None]
-    bias_prev = jnp.take(keep_bias, picked, axis=0)[:, None]
-    mixed = spatial(
-        slots, video, gain_spatial[None], qkv_spatial, out_spatial, bias_first, bias_prev,
-        devices, toks, scale,
-    )
-
+    slots = jnp.stack([slots, picked // frames, picked % frames])
+    own_reg = regions.astype(jnp.float32)[:, None]
+    mixed, known = spatial(
+        slots, video, gain_spatial[None], qkv_spatial, out_spatial, own_reg, devices, toks, scale
+    )
     width = 16 if places % (devices * 16) == 0 else places // devices
     part = devices * width
     chunks = places // part
-    my_open = (regions_all != 2).astype(jnp.float32)
-    base = lax.axis_index("tok") * places + lax.axis_index("frame") * width
-    gain_row = gain_temporal[None]
-    done = []
-    for c in range(chunks):
-        rows = lax.all_to_all(
-            mixed[:, c * part : (c + 1) * part], "frame", split_axis=1, concat_axis=0, tiled=True
-        )
-        open_row = lax.dynamic_slice_in_dim(my_open, base + c * part, width, axis=1)
-        finished = temporal(
-            rows.reshape(total_frames * width, feature),
-            open_row.reshape(1, total_frames * width),
-            gain_row, qkv_temporal, out_temporal, width, scale,
-        )
-        done.append(
-            lax.all_to_all(
-                finished.reshape(total_frames, width, feature),
-                "frame", split_axis=0, concat_axis=1, tiled=True,
-            )
-        )
-    return jnp.concatenate(done, axis=1)
+    is_open = (known.reshape(total_frames, places) != 2).astype(jnp.float32)
+    base = lax.axis_index("frame") * width
+    open_rows = jnp.stack(
+        [
+            lax.dynamic_slice_in_dim(is_open, base + c * part, width, axis=1).reshape(1, -1)
+            for c in range(chunks)
+        ]
+    )
+    return temporal(
+        mixed, open_rows, gain_temporal[None], qkv_temporal, out_temporal, devices, width, scale
+    )
 
 
 def solution(mesh):

time: 204 us -> 161 us (0.79); the launches traced: 200 us -> 161 us
  Pallas kernels: 115 us -> 152 us
  starting transfers between devices: 29.4 us -> 0 us
  waiting for transfers between devices: 24.7 us -> 0 us
  blocking collectives: 16.3 us -> 0 us
  local copies, waits for them, and re-layouts: 10.5 us -> 5.8 us
    pallas_call x2 -> x1, Pallas kernels: 29.7 us -> 68 us  [temporal(): pl.pallas_call(functools.partial(temporal_kernel, devices=devices, width=...]
    all_to_all x4 -> x0, starting transfers between devices: 29.4 us -> none  [the longest x2 17.4 us: shards(): lax.all_to_all(mixed[:, c * part:(c + 1) * part], 'frame', split_axis=1,...]
    all_to_all x4 -> x0, waiting for transfers between devices: 24.7 us -> none  [the longest x2 12.7 us: shards(): lax.all_to_all(finished.reshape(total_frames, width, feature), 'frame', s...]
    all_gather x1 -> x0, blocking collectives: 16.3 us -> none  [shards(): regions_all = lax.all_gather(regions, ('frame', 'tok'), axis=0, tiled=False)]
    slice x3 -> x0, local copies, waits for them, and re-layouts: 4.18 us -> none  [shards(): mixed[:, c * part:(c + 1) * part]]
    unnamed x4 -> x1, local copies, waits for them, and re-layouts: 0.01 us -> 2.37 us
  transfers between devices with their start and end apart: 4 -> 0, of which waited for: 2 -> 0; matrix products, arithmetic and copies ran while one was open for 3% -> 0% of each run, Pallas kernels for 15% -> 0%
where the time goes in v3:
time: 161 us
  Pallas kernels  152 us (94%)
  local copies, waits for them, and re-layouts  5.8 us (4%)
  other arithmetic  3.36 us (2%)
    pallas_call x1, Pallas kernels, spatial(): pl.pallas_call(functools.partial(spatial_kernel, devices=devices, scale=s...  83.8 us
    pallas_call x1, Pallas kernels, temporal(): pl.pallas_call(functools.partial(temporal_kernel, devices=devices, width=...  68 us

profile of v3, /device:TPU:16, one launch (start us, length us, event | category | flops | bytes accessed | tf_op | source)
XLA Modules:
  0.0 161.0 jit_solution(15581252464716931520)
XLA Ops:
  0.0 0.7 fusion.2
  0.7 0.6 pad_add_fusion.slots_ref
  1.3 0.7 convert_element_type.9
  2.0 0.6 broadcast_in_dim.10.own_reg_ref
  2.6 1.3 broadcast_in_dim.9.gain_ref
  3.9 1.3 broadcast_in_dim.11.gain_ref
  5.2 83.8 %shard_map.91 = (bf16[2,256,1152]{2,1,0:T(8,128)(2,1)}, f32[8,2,1,256]{3,2,1,0:T(1,128)}) custom-call(s32[3,2]{1,0:T(4,128)} %pad_add_fusion.slots_ref, bf16[2,256,1152]{2,1,0:T(8,128)(2,1)} %video_ref.1, f32[1,1152]{1,0:T(1,128)} %broadcast_in_dim.9.gain_ref, bf16[1152,3456]{1,0:T(8,128)(2,1)} %wqkv_ref.2, bf16[1152,1152]{1,0:T(8,128)(2,1)} %wout_ref.2, ...), custom_call_target="tpu_custom_call" | custom-call | flops 12884901888 | bytes 20971520 | tf_op jit(solution)/shard_map/pallas_call | solution.py:266
  89.0 0.8 fusion
  89.8 0.1 constant_dynamic-slice_fusion.1
  89.8 0.1 stack_reshape.6
  89.9 0.1 stack_reshape.7
  90.0 0.6 pad_maximum_fusion.open_ref
  90.6 68.0 %shard_map.92 = bf16[2,256,1152]{2,1,0:T(8,128)(2,1)} custom-call(bf16[2,256,1152]{2,1,0:T(8,128)(2,1)} %get-tuple-element.7.mixed_ref, f32[2,1,256]{2,1,0:T(1,128)} %pad_maximum_fusion.open_ref, f32[1,1152]{1,0:T(1,128)} %broadcast_in_dim.11.gain_ref, bf16[1152,3456]{1,0:T(8,128)(2,1)} %wqkv_ref.3, bf16[1152,1152]{1,0:T(8,128)(2,1)} %wout_ref.3), custom_call_target="tpu_custom_call" | custom-call | flops 5435817984 | bytes 16777216 | tf_op jit(solution)/shard_map/pallas_call | solution.py:416
  158.6 2.4 %copy.12 = bf16[2,256,1152]{2,1,0:T(8,128)(2,1)} copy(bf16[2,256,1152]{2,1,0:T(8,128)(2,1)} %shard_map.92) | data formatting | bytes 2359296
  (2 shorter events, 0.0 us)

commit v4 on v3

--- a/solution.py
+++ b/solution.py
@@ -167,17 +167,17 @@
 
     @pl.when(me > 0)
     def _():
+        for k in range(1, devices):
+            arrival(lax.rem(me + k, devices)).wait_recv()
+
+    send_kv(first_ref[...], rem_ref, frames, 2 * frames)
+
+    @pl.when(me > 0)
+    def _():
         shift.wait_recv()
 
     for f in range(frames):
         send_kv(tail_ref[f], rem_ref, f, frames + f)
-
-    @pl.when(me > 0)
-    def _():
-        for k in range(1, devices):
-            arrival(lax.rem(me + k, devices)).wait_recv()
-
-    send_kv(first_ref[...], rem_ref, frames, 2 * frames)
 
     for f in range(frames):
         swap(own_ref, f, f).wait()
@@ -229,12 +229,12 @@
             ) / total
             att_ref[:, cols] = jnp.where(inside, o.astype(jnp.bfloat16), att_ref[:, cols])
 
-        def pair(i, _):
-            one(2 * i)
-            one(2 * i + 1)
+        def group(i, _):
+            for extra in range(4):
+                one(4 * i + extra)
             return 0
 
-        lax.fori_loop(0, HEADS // 2, pair, 0)
+        lax.fori_loop(0, HEADS // 4, group, 0)
         out_ref[frame] = (
             video_ref[frame].astype(jnp.float32)
             + jnp.dot(att_ref[...], wout_ref[...], preferred_element_type=jnp.float32)
@@ -331,12 +331,12 @@
         ) / jnp.sum(p, axis=-1, keepdims=True)
         att_ref[:, cols] = jnp.where(inside, o.astype(jnp.bfloat16), att_ref[:, cols])
 
-    def pair(k, _):
-        one(2 * k)
-        one(2 * k + 1)
+    def group(k, _):
+        for extra in range(4):
+            one(4 * k + extra)
         return 0
 
-    lax.fori_loop(0, HEADS // 2, pair, 0)
+    lax.fori_loop(0, HEADS // 4, group, 0)
     return (
         rows.astype(jnp.float32)
         + jnp.dot(att_ref[...], wout_ref[...], preferred_element_type=jnp.float32)

time: 161 us -> 160 us (level); the launches traced: 161 us -> 157 us
  Pallas kernels: 152 us -> 148 us
    pallas_call x1, Pallas kernels: 68 us -> 65.7 us  [temporal(): pl.pallas_call(functools.partial(temporal_kernel, devices=devices, width=...]
where the time goes in v4:
time: 160 us; the launch traced here: 157 us
  Pallas kernels  148 us (92%)
  local copies, waits for them, and re-layouts  5.8 us (4%)
  other arithmetic  3.36 us (2%)
    pallas_call x1, Pallas kernels, spatial(): pl.pallas_call(functools.partial(spatial_kernel, devices=devices, scale=s...  82.4 us
    pallas_call x1, Pallas kernels, temporal(): pl.pallas_call(functools.partial(temporal_kernel, devices=devices, width=...  65.7 us

profile of v4, /device:TPU:16, one launch (start us, length us, event | category | flops | bytes accessed | tf_op | source)
XLA Modules:
  0.0 157.3 jit_solution(15748825239033988938)
XLA Ops:
  0.0 0.7 fusion.2
  0.7 0.6 pad_add_fusion.slots_ref
  1.3 0.7 convert_element_type.9
  2.0 0.6 broadcast_in_dim.10.own_reg_ref
  2.6 1.3 broadcast_in_dim.9.gain_ref
  3.9 1.3 broadcast_in_dim.11.gain_ref
  5.2 82.4 %shard_map.91 = (bf16[2,256,1152]{2,1,0:T(8,128)(2,1)}, f32[8,2,1,256]{3,2,1,0:T(1,128)}) custom-call(s32[3,2]{1,0:T(4,128)} %pad_add_fusion.slots_ref, bf16[2,256,1152]{2,1,0:T(8,128)(2,1)} %video_ref.1, f32[1,1152]{1,0:T(1,128)} %broadcast_in_dim.9.gain_ref, bf16[1152,3456]{1,0:T(8,128)(2,1)} %wqkv_ref.2, bf16[1152,1152]{1,0:T(8,128)(2,1)} %wout_ref.2, ...), custom_call_target="tpu_custom_call" | custom-call | flops 12884901888 | bytes 20971520 | tf_op jit(solution)/shard_map/pallas_call | solution.py:266
  87.6 0.8 fusion
  88.4 0.1 constant_dynamic-slice_fusion.1
  88.5 0.1 stack_reshape.6
  88.6 0.1 stack_reshape.7
  88.6 0.6 pad_maximum_fusion.open_ref
  89.2 65.7 %shard_map.92 = bf16[2,256,1152]{2,1,0:T(8,128)(2,1)} custom-call(bf16[2,256,1152]{2,1,0:T(8,128)(2,1)} %get-tuple-element.7.mixed_ref, f32[2,1,256]{2,1,0:T(1,128)} %pad_maximum_fusion.open_ref, f32[1,1152]{1,0:T(1,128)} %broadcast_in_dim.11.gain_ref, bf16[1152,3456]{1,0:T(8,128)(2,1)} %wqkv_ref.3, bf16[1152,1152]{1,0:T(8,128)(2,1)} %wout_ref.3), custom_call_target="tpu_custom_call" | custom-call | flops 5435817984 | bytes 16777216 | tf_op jit(solution)/shard_map/pallas_call | solution.py:416
  154.9 2.4 %copy.12 = bf16[2,256,1152]{2,1,0:T(8,128)(2,1)} copy(bf16[2,256,1152]{2,1,0:T(8,128)(2,1)} %shard_map.92) | data formatting | bytes 2359296
  (2 shorter events, 0.0 us)
